TPU v7x, 32 devices: a whole 2x2x4 slice. The times are simulated.
32 devices in a mesh: space: 8 (over z, x), chan: 4 (over y, core).
Axes of the slice: x: 2, y: 2, z: 4, core: 2. Of those that a mesh axis runs over, the one named last changes fastest.
Arguments:
- features: bfloat16 [1024, 512], P('space', 'chan'), may hold values from -6 to 6
- mask: int32 [1024], P('space'), may hold values 0 or 1
- rulebook: int32 [16, 27], P('space'), may hold values from -1 to 15, as said below
- weight_first: bfloat16 [512, 27, 512], P('space', None, 'chan'), may hold values from -0.0546875 to 0.0546875
- weight_second: bfloat16 [512, 27, 512], P('space', None, 'chan'), may hold values from -0.0546875 to 0.0546875
- cotangent: bfloat16 [1024, 512], P('space', 'chan'), may hold values from -6 to 6
Outputs:
- output: bfloat16 [1024, 512], P('space', 'chan')
- features_grad: bfloat16 [1024, 512], P('space', 'chan')
- weight_first_grad: float32 [512, 27, 512], P('space', None, 'chan')
- weight_second_grad: float32 [512, 27, 512], P('space', None, 'chan')
Inputs may be any that keep to these rules, and one draw needn't show every extreme that they name: `rulebook`: entry [b, c] is the brick that feeds brick b through brick offset c, or -1 for none; entry 13 is b itself. A brick of another device belongs to a device s one or two indices away; if it feeds the device s + 1, s + 2, s - 1 or s - 2 (k = 0, 1, 2, 3 respectively), it is brick s * 2 + ((k + h) mod 2) for some h below 1.
All inputs are finite; a program needn't handle non-finite values. No bound on the sum of `mask` on one device may be relied on, other than what follows from the above.
Results may differ from a plain program's by a relative error of at most 0.005.
Values may be sent and summed in bfloat16 or wider, within the bound.
A program may use at most 128 MiB of HBM per device.

v0:
```python
import jax
import jax.numpy as jnp
import numpy as np
from jax import lax
from jax.sharding import PartitionSpec as P

HB = 1


direction_steps = (1, 2, -1, -2)


def passed_along(value, axis, by):
    devices = lax.axis_size(axis)
    pairs = [(i, i + by) for i in range(devices) if 0 <= i + by < devices]
    return lax.ppermute(value, axis, pairs)


def offset_tables():
    brick_table = np.zeros((27, 64), np.int32)
    cell_table = np.zeros((27, 64), np.int32)
    for offset in range(27):
        moves = (offset // 9 - 1, offset // 3 % 3 - 1, offset % 3 - 1)
        for voxel in range(64):
            cells = (voxel // 16, voxel // 4 % 4, voxel % 4)
            target = [cells[axis_number] + moves[axis_number] for axis_number in range(3)]
            brick_table[offset, voxel] = (
                (target[0] // 4 + 1) * 9 + (target[1] // 4 + 1) * 3 + (target[2] // 4 + 1)
            )
            cell_table[offset, voxel] = target[0] % 4 * 16 + target[1] % 4 * 4 + target[2] % 4
    return (brick_table, cell_table)


def on_device(features, mask, rulebook, weight_first, weight_second, cotangent):
    brick_table, cell_table = offset_tables()
    bricks = rulebook.shape[0]
    spread = HB
    row_count = features.shape[0]
    halo_rows = 4 * spread * 64
    device_index = lax.axis_index("space")
    owner_device = rulebook // bricks
    within = rulebook % bricks
    sources = device_index - jnp.array(direction_steps, jnp.int32)
    lent_table = (
        jnp.arange(4, dtype=jnp.int32)[:, None] * spread
        + jnp.arange(spread, dtype=jnp.int32)[None, :]
    ) % bricks
    matches = (owner_device[:, :, None, None] == sources[None, None, :, None]) & (
        within[:, :, None, None] == lent_table[None, None]
    )
    numbers = bricks + jnp.arange(4 * spread, dtype=jnp.int32).reshape(4, spread)
    remote = jnp.sum(jnp.where(matches, numbers, 0), axis=(2, 3))
    slot_index = jnp.where(
        rulebook < 0, bricks + 4 * spread, jnp.where(owner_device == device_index, within, remote)
    )
    lookup = slot_index[:, brick_table] * 64 + cell_table[None]
    lookup = jnp.transpose(lookup, (1, 0, 2)).reshape(27, row_count).astype(jnp.int32)
    active = mask.astype(jnp.float32)[:, None]
    masked = (features.astype(jnp.float32) * active).astype(jnp.bfloat16)

    def outgoing(source, position):
        shaped = source.reshape(bricks, 64, source.shape[1])
        return jnp.take(shaped, lent_table[position], axis=0).reshape(spread * 64, source.shape[1])

    def extend(source):
        gathered = lax.all_gather(source, "chan", axis=1, tiled=True)
        blocks = [gathered]
        for position, offset in enumerate(direction_steps):
            blocks.append(passed_along(outgoing(gathered, position), "space", offset))
        blocks.append(jnp.zeros((64, gathered.shape[1]), jnp.bfloat16))
        return jnp.concatenate(blocks, 0)

    def lend_back(own_rows, returned, position):
        shaped = own_rows.reshape(bricks, 64, own_rows.shape[1])
        shaped = shaped.at[lent_table[position]].add(
            returned.reshape(spread, 64, own_rows.shape[1])
        )
        return shaped.reshape(row_count, own_rows.shape[1])

    def settle(running):
        summed = lax.psum_scatter(
            running[: row_count + halo_rows], "chan", scatter_dimension=1, tiled=True
        )
        own_rows = summed[:row_count]
        for position, offset in enumerate(direction_steps):
            block_start = row_count + position * spread * 64
            returned = passed_along(
                summed[block_start : block_start + spread * 64], "space", -offset
            )
            own_rows = lend_back(own_rows, returned, position)
        return own_rows

    def weight_term(extended, gradient):

        def advance(offset):
            picked = jnp.take(extended, lookup[offset], axis=0)
            return lax.dot_general(
                picked, gradient, (((0,), (0,)), ((), ())), preferred_element_type=jnp.float32
            )

        stacked = lax.map(advance, jnp.arange(27, dtype=jnp.int32))
        return jnp.transpose(stacked, (1, 0, 2))

    ext_in = extend(masked)
    table_rows = ext_in.shape[0]
    width = ext_in.shape[1]
    initial = jnp.zeros((row_count, weight_first.shape[2]), jnp.float32)
    segment = lax.all_gather(weight_first, "space", axis=0, tiled=True)
    columns = ext_in

    def advance(offset, running):
        picked = jnp.take(columns, lookup[offset], axis=0)
        kernel = lax.dynamic_index_in_dim(segment, offset, 1, keepdims=False)
        return running + jnp.dot(picked, kernel, preferred_element_type=jnp.float32)

    first_act = active * lax.fori_loop(0, 27, advance, initial)
    hidden = jax.nn.silu(first_act).astype(jnp.bfloat16)
    ext_hidden = extend(hidden)
    second_whole = lax.all_gather(weight_second, "space", axis=0, tiled=True)

    def forward_step(offset, running):
        picked = jnp.take(ext_hidden, lookup[offset], axis=0)
        kernel = lax.dynamic_index_in_dim(second_whole, offset, 1, keepdims=False)
        return running + jnp.dot(picked, kernel, preferred_element_type=jnp.float32)

    second_act = active * lax.fori_loop(
        0, 27, forward_step, jnp.zeros((row_count, second_whole.shape[2]), jnp.float32)
    )
    output = second_act.astype(jnp.bfloat16)
    grad_second = (cotangent.astype(jnp.float32) * active).astype(jnp.bfloat16)
    weight_second_grad = lax.psum_scatter(
        weight_term(ext_hidden, grad_second), "space", scatter_dimension=0, tiled=True
    )

    def backward_step(offset, running):
        kernel = lax.dynamic_index_in_dim(second_whole, offset, 1, keepdims=False)
        contrib = lax.dot_general(
            grad_second, kernel, (((1,), (1,)), ((), ())), preferred_element_type=jnp.float32
        )
        return running.at[lookup[offset]].add(contrib)

    hidden_grad = settle(
        lax.fori_loop(0, 27, backward_step, jnp.zeros((table_rows, width), jnp.float32))
    )
    sigmoid_first = jax.nn.sigmoid(first_act)
    grad_first = (
        active * hidden_grad * sigmoid_first * (1.0 + first_act * (1.0 - sigmoid_first))
    ).astype(jnp.bfloat16)
    weight_first_grad = lax.psum_scatter(
        weight_term(ext_in, grad_first), "space", scatter_dimension=0, tiled=True
    )

    def add_back(running, segment):
        columns = running

        def advance(offset, current):
            kernel = lax.dynamic_index_in_dim(segment, offset, 1, keepdims=False)
            contrib = lax.dot_general(
                grad_first, kernel, (((1,), (1,)), ((), ())), preferred_element_type=jnp.float32
            )
            return current.at[lookup[offset]].add(contrib)

        columns = lax.fori_loop(0, 27, advance, columns)
        return columns

    running = add_back(
        jnp.zeros((table_rows, width), jnp.float32),
        lax.all_gather(weight_first, "space", axis=0, tiled=True),
    )
    features_grad = (active * settle(running)).astype(jnp.bfloat16)
    return (output, features_grad, weight_first_grad, weight_second_grad)


def solution(mesh):
    placed = (
        P("space", "chan"),
        P("space"),
        P("space", None),
        P("space", None, "chan"),
        P("space", None, "chan"),
        P("space", "chan"),
    )
    return jax.shard_map(
        on_device,
        mesh=mesh,
        in_specs=placed,
        out_specs=(
            P("space", "chan"),
            P("space", "chan"),
            P("space", None, "chan"),
            P("space", None, "chan"),
        ),
        check_vma=False,
    )
```

profile of v0, /device:TPU:0, one launch (start us, length us, event | category | flops | bytes accessed | tf_op | source)
XLA Modules:
  0.0 806.0 jit_solution(12813697960733483102)
XLA Ops:
  11.2 3.3 gather_fusion.4
  16.8 61.3 %all-gather.5.cloned.1.call-done = bf16[512,27,128]{2,0,1:T(8,128)(2,1)} async-done(((bf16[64,27,128]{2,0,1:T(8,128)(2,1)}), bf16[512,27,128]{2,0,1:T(8,128)(2,1)}) %all-gather.5.cloned.1.call-update) | async-done | bytes 3538960 | tf_op jit(solution)/shard_map/all_gather | solution.py:119
  78.2 80.3 %while.83 = (s32[]{:T(128)}, f32[448,512]{1,0:T(8,128)S(1)}, s32[27,128]{1,0:T(8,128)S(1)}, bf16[512,27,128]{2,0,1:T(8,128)(2,1)}, bf16[128,128]{1,0:T(8,128)(2,1)S(1)}, /*index=5*/s32[]{:T(128)}) while((s32[]{:T(128)}, f32[448,512]{1,0:T(8,128)S(1)}, s32[27,128]{1,0:T(8,128)S(1)}, bf16[512,27,128]{2,0,1:T(8,128)(2,1)}, ...), condition=%wide.region_7.10_spmd, body=%wide.region_5.9_spmd.sunk | while | flops 16843136 | bytes 1738325 | solution.py:143
  79.5 1.7 scatter_fusion
  82.5 1.7 scatter_fusion
  85.4 1.7 scatter_fusion
  91.4 1.7 scatter_fusion
  97.3 1.7 scatter_fusion
  100.3 1.7 scatter_fusion
  106.2 1.7 scatter_fusion
  168.6 5.4 all_gather.13
  176.7 5.2 collective-permute-start.1
  181.9 3.9 collective-permute-start
  190.0 59.1 %all-gather.3.cloned.1.call-done = bf16[512,27,128]{2,0,1:T(8,128)(2,1)} async-done(((bf16[64,27,128]{2,0,1:T(8,128)(2,1)}), bf16[512,27,128]{2,0,1:T(8,128)(2,1)}) %all-gather.3.cloned.1.call-update) | async-done | bytes 3538960 | tf_op jit(solution)/shard_map/all_gather | solution.py:108
  249.0 55.7 %while.87 = (s32[]{:T(128)}, f32[128,128]{1,0:T(8,128)S(1)}, s32[27,128]{1,0:T(8,128)S(1)}, bf16[448,512]{1,0:T(8,128)(2,1)S(1)}, bf16[512,27,128]{2,0,1:T(8,128)(2,1)}, /*index=5*/s32[]{:T(128)}, s32[]{:T(128)}) while((s32[]{:T(128)}, f32[128,128]{1,0:T(8,128)S(1)}, s32[27,128]{1,0:T(8,128)S(1)}, bf16[448,512]{1,0:T(8,128)(2,1)S(1)}, ...), condition=%wide.region_2.5_spmd.clone, body=%wide.region_1.4_spmd.clone.sunk | while | flops 16877316 | bytes 661863 | solution.py:116
  304.7 3.2 collective-permute-start.11
  307.9 2.5 collective-permute-start.10
  312.3 3.8 collective-permute-done.9
  318.3 80.3 %while.84 = (s32[]{:T(128)}, f32[448,512]{1,0:T(8,128)S(1)}, s32[27,128]{1,0:T(8,128)S(1)}, bf16[512,27,128]{2,0,1:T(8,128)(2,1)}, bf16[128,128]{1,0:T(8,128)(2,1)S(1)}, /*index=5*/s32[]{:T(128)}) while((s32[]{:T(128)}, f32[448,512]{1,0:T(8,128)S(1)}, s32[27,128]{1,0:T(8,128)S(1)}, bf16[512,27,128]{2,0,1:T(8,128)(2,1)}, ...), condition=%wide.region_15.18_spmd, body=%wide.region_13.17_spmd.sunk | while | flops 16843136 | bytes 1738325 | solution.py:163
  399.7 3.7 broadcast.332.clone
  403.3 119.0 %while.85 = (s32[]{:T(128)}, f32[27,512,128]{2,1,0:T(8,128)}, s32[27]{0:T(128)S(1)}, s32[27,128]{1,0:T(8,128)S(1)}, bf16[448,512]{1,0:T(8,128)(2,1)S(1)}, /*inde...) while((s32[]{:T(128)}, f32[27,512,128]{2,1,0:T(8,128)}, s32[27]{0:T(128)S(1)}, ...), condition=%wide.region_18.21_spmd, body=%wide.region_17.20_spmd.sunk | while | flops 16844548 | bytes 694683 | solution.py:101
  522.4 5.4 all_gather.15
  530.5 6.0 collective-permute-start.5
  536.5 3.1 collective-permute-start.4
  539.7 1.9 collective-permute-done.4
  541.6 3.7 broadcast.332.clone.1
  545.4 119.1 %while.86 = (s32[]{:T(128)}, f32[27,512,128]{2,1,0:T(8,128)}, s32[27]{0:T(128)S(1)}, s32[27,128]{1,0:T(8,128)S(1)}, bf16[448,512]{1,0:T(8,128)(2,1)S(1)}, /*inde...) while((s32[]{:T(128)}, f32[27,512,128]{2,1,0:T(8,128)}, s32[27]{0:T(128)S(1)}, ...), condition=%wide.region_21.24_spmd, body=%wide.region_20.23_spmd.sunk | while | flops 16844548 | bytes 694683 | solution.py:101
  666.7 55.8 %while.88 = (s32[]{:T(128)}, f32[128,128]{1,0:T(8,128)S(1)}, s32[27,128]{1,0:T(8,128)S(1)}, bf16[448,512]{1,0:T(8,128)(2,1)S(1)}, bf16[512,27,128]{2,0,1:T(8,128)(2,1)}, /*index=5*/s32[]{:T(128)}, s32[]{:T(128)}) while((s32[]{:T(128)}, f32[128,128]{1,0:T(8,128)S(1)}, s32[27,128]{1,0:T(8,128)S(1)}, bf16[448,512]{1,0:T(8,128)(2,1)S(1)}, ...), condition=%wide.region_4.7_spmd.clone, body=%wide.region_3.6_spmd.clone.sunk | while | flops 16877316 | bytes 661863 | solution.py:126
  722.6 8.9 %collective-permute-start.15 = (f32[64,128]{1,0:T(8,128)S(1)}, f32[64,128]{1,0:T(8,128)S(1)}, u32[]{:S(2)}, u32[]{:S(2)}) collective-permute-start(f32[64,128]{1,0:T(8,128)S(1)} %get-tuple-element.671), channel_id=1, source_target_pairs={{0,8},{4,12},{8,16},{12,20},{16,24},{20,28},{1,9},{5,13},{9,17},{1... | collective-permute-start | bytes 98312 | tf_op jit(solution)/shard_map/ppermute | solution.py:16
  731.5 4.0 collective-permute-start.14
  737.5 3.9 collective-permute-done.13
  744.0 55.2 %reduce-scatter.11.cloned.1.call-done = f32[64,27,128]{2,0,1:T(8,128)} async-done(((f32[512,27,128]{2,0,1:T(8,128)}), f32[64,27,128]{2,0,1:T(8,128)}) %reduce-scatter.11.cloned.1.call-update) | async-done | bytes 884752 | tf_op jit(solution)/shard_map/reduce_scatter | solution.py:131
  (790 shorter events, 417.8 us)
Async XLA Ops:
  7.2 70.9 %all-gather.5.cloned.1.call-start = ((), (), s32[]{:S(2)}) async-start(), calls=%async_computation.5 | async-start | bytes 3981312 | tf_op jit(solution)/shard_map/all_gather | solution.py:119
  7.9 179.9 %reduce-scatter.5.cloned.1.call-start = ((), (), s32[]{:S(2)}) async-start(), calls=%async_computation.6 | async-start | bytes 983040 | tf_op jit(solution)/shard_map/reduce_scatter | solution.py:81
  78.2 107.6 %copy-start = (s32[3]{0:T(128)S(1)}, s32[3]{0:T(128)}, u32[]{:S(2)}) copy-start(s32[3]{0:T(128)} %constant.387.clone.1) | copy-start | bytes 40
  159.4 89.6 %all-gather.3.cloned.1.call-start = ((), (), s32[]{:S(2)}) async-start(), calls=%async_computation.4 | async-start | bytes 3981312 | tf_op jit(solution)/shard_map/all_gather | solution.py:108
  160.2 504.4 %reduce-scatter.7.cloned.1.call-start = ((), (), s32[]{:S(2)}) async-start(), calls=%async_computation.7 | async-start | bytes 983040 | tf_op jit(solution)/shard_map/reduce_scatter | solution.py:81
  174.1 13.7 %collective-permute-start.3 = (bf16[64,512]{1,0:T(8,128)(2,1)S(1)}, bf16[64,512]{1,0:T(8,128)(2,1)S(1)}, u32[]{:S(2)}, u32[]{:S(2)}) collective-permute-start(bf16[64,512]{1,0:T(8,128)(2,1)S(1)} %get-tuple-element.683), channel_id=1, source_target_pairs={{8,0},{12,4},{16,8},{20,12},{24,16},{28,20},{9,1},{13,5},{17,9},{2... | collective-permute-start | bytes 196616 | tf_op jit(solution)/shard_map/ppermute | solution.py:16
  175.4 12.3 %collective-permute-start.2 = (bf16[64,512]{1,0:T(8,128)(2,1)S(1)}, bf16[64,512]{1,0:T(8,128)(2,1)S(1)}, u32[]{:S(2)}, u32[]{:S(2)}) collective-permute-start(bf16[64,512]{1,0:T(8,128)(2,1)S(1)} %get-tuple-element.684), channel_id=1, source_target_pairs={{4,0},{8,4},{12,8},{16,12},{20,16},{24,20},{28,24},{5,1},{9,5},{13... | collective-permute-start | bytes 196616 | tf_op jit(solution)/shard_map/ppermute | solution.py:16
  176.7 11.0 %collective-permute-start.1 = (bf16[64,512]{1,0:T(8,128)(2,1)S(1)}, bf16[64,512]{1,0:T(8,128)(2,1)S(1)}, u32[]{:S(2)}, u32[]{:S(2)}) collective-permute-start(bf16[64,512]{1,0:T(8,128)(2,1)S(1)} %get-tuple-element.685), channel_id=1, source_target_pairs={{0,8},{4,12},{8,16},{12,20},{16,24},{20,28},{1,9},{5,13},{9,17},{1... | collective-permute-start | bytes 196616 | tf_op jit(solution)/shard_map/ppermute | solution.py:16
  181.9 5.8 collective-permute-start
  187.8 123.9 %slice-start.1 = ((f32[384,128]{1,0:T(8,128)}), f32[128,128]{1,0:T(8,128)S(1)}, s32[]{:S(2)}) async-start(f32[384,128]{1,0:T(8,128)} %reduce-scatter.5.cloned.1.call-done), calls=%async_computation.11 | async-start | bytes 131072 | tf_op jit(solution)/shard_map/slice | solution.py:84
  188.7 123.0 %collective-permute-start.8 = (f32[64,128]{1,0:T(8,128)S(1)}, f32[64,128]{1,0:T(8,128)S(1)}, u32[]{:S(2)}, u32[]{:S(2)}) collective-permute-start(f32[64,128]{1,0:T(8,128)S(1)} %get-tuple-element.678), channel_id=1, source_target_pairs={{4,0},{8,4},{12,8},{16,12},{20,16},{24,20},{28,24},{5,1},{9,5},{13... | collective-permute-start | bytes 98312 | tf_op jit(solution)/shard_map/ppermute | solution.py:16
  304.7 12.8 %collective-permute-start.11 = (f32[64,128]{1,0:T(8,128)S(1)}, f32[64,128]{1,0:T(8,128)S(1)}, u32[]{:S(2)}, u32[]{:S(2)}) collective-permute-start(f32[64,128]{1,0:T(8,128)S(1)} %get-tuple-element.675), channel_id=1, source_target_pairs={{0,8},{4,12},{8,16},{12,20},{16,24},{20,28},{1,9},{5,13},{9,17},{1... | collective-permute-start | bytes 98312 | tf_op jit(solution)/shard_map/ppermute | solution.py:16
  307.9 8.9 %collective-permute-start.10 = (f32[64,128]{1,0:T(8,128)S(1)}, f32[64,128]{1,0:T(8,128)S(1)}, u32[]{:S(2)}, u32[]{:S(2)}) collective-permute-start(f32[64,128]{1,0:T(8,128)S(1)} %get-tuple-element.676), channel_id=1, source_target_pairs={{0,4},{4,8},{8,12},{12,16},{16,20},{20,24},{24,28},{1,5},{5,9},{9,... | collective-permute-start | bytes 98312 | tf_op jit(solution)/shard_map/ppermute | solution.py:16
  310.3 5.8 collective-permute-start.9
  399.6 344.4 %reduce-scatter.9.cloned.1.call-start = ((), (), s32[]{:S(2)}) async-start(), calls=%async_computation.8 | async-start | bytes 7962624 | tf_op jit(solution)/shard_map/reduce_scatter | solution.py:149
  522.4 276.8 %reduce-scatter.11.cloned.1.call-start = ((), (), s32[]{:S(2)}) async-start(), calls=%async_computation.9 | async-start | bytes 7962624 | tf_op jit(solution)/shard_map/reduce_scatter | solution.py:131
  527.9 13.7 %collective-permute-start.7 = (bf16[64,512]{1,0:T(8,128)(2,1)S(1)}, bf16[64,512]{1,0:T(8,128)(2,1)S(1)}, u32[]{:S(2)}, u32[]{:S(2)}) collective-permute-start(bf16[64,512]{1,0:T(8,128)(2,1)S(1)} %get-tuple-element.679), channel_id=1, source_target_pairs={{8,0},{12,4},{16,8},{20,12},{24,16},{28,20},{9,1},{13,5},{17,9},{2... | collective-permute-start | bytes 196616 | tf_op jit(solution)/shard_map/ppermute | solution.py:16
  529.2 12.4 %collective-permute-start.6 = (bf16[64,512]{1,0:T(8,128)(2,1)S(1)}, bf16[64,512]{1,0:T(8,128)(2,1)S(1)}, u32[]{:S(2)}, u32[]{:S(2)}) collective-permute-start(bf16[64,512]{1,0:T(8,128)(2,1)S(1)} %get-tuple-element.680), channel_id=1, source_target_pairs={{4,0},{8,4},{12,8},{16,12},{20,16},{24,20},{28,24},{5,1},{9,5},{13... | collective-permute-start | bytes 196616 | tf_op jit(solution)/shard_map/ppermute | solution.py:16
  530.5 11.0 %collective-permute-start.5 = (bf16[64,512]{1,0:T(8,128)(2,1)S(1)}, bf16[64,512]{1,0:T(8,128)(2,1)S(1)}, u32[]{:S(2)}, u32[]{:S(2)}) collective-permute-start(bf16[64,512]{1,0:T(8,128)(2,1)S(1)} %get-tuple-element.681), channel_id=1, source_target_pairs={{0,8},{4,12},{8,16},{12,20},{16,24},{20,28},{1,9},{5,13},{9,17},{1... | collective-permute-start | bytes 196616 | tf_op jit(solution)/shard_map/ppermute | solution.py:16
  536.5 5.0 collective-permute-start.4
  664.6 72.3 %slice-start = ((f32[384,128]{1,0:T(8,128)}), f32[128,128]{1,0:T(8,128)S(1)}, s32[]{:S(2)}) async-start(f32[384,128]{1,0:T(8,128)} %reduce-scatter.7.cloned.1.call-done), calls=%async_computation.10 | async-start | bytes 131072 | tf_op jit(solution)/shard_map/slice | solution.py:84
  665.4 71.4 %collective-permute-start.12 = (f32[64,128]{1,0:T(8,128)S(1)}, f32[64,128]{1,0:T(8,128)S(1)}, u32[]{:S(2)}, u32[]{:S(2)}) collective-permute-start(f32[64,128]{1,0:T(8,128)S(1)} %get-tuple-element.674), channel_id=1, source_target_pairs={{4,0},{8,4},{12,8},{16,12},{20,16},{24,20},{28,24},{5,1},{9,5},{13... | collective-permute-start | bytes 98312 | tf_op jit(solution)/shard_map/ppermute | solution.py:16
  722.6 20.2 %collective-permute-start.15 = (f32[64,128]{1,0:T(8,128)S(1)}, f32[64,128]{1,0:T(8,128)S(1)}, u32[]{:S(2)}, u32[]{:S(2)}) collective-permute-start(f32[64,128]{1,0:T(8,128)S(1)} %get-tuple-element.671), channel_id=1, source_target_pairs={{0,8},{4,12},{8,16},{12,20},{16,24},{20,28},{1,9},{5,13},{9,17},{1... | collective-permute-start | bytes 98312 | tf_op jit(solution)/shard_map/ppermute | solution.py:16
  731.5 10.5 %collective-permute-start.14 = (f32[64,128]{1,0:T(8,128)S(1)}, f32[64,128]{1,0:T(8,128)S(1)}, u32[]{:S(2)}, u32[]{:S(2)}) collective-permute-start(f32[64,128]{1,0:T(8,128)S(1)} %get-tuple-element.672), channel_id=1, source_target_pairs={{0,4},{4,8},{8,12},{12,16},{16,20},{20,24},{24,28},{1,5},{5,9},{9,... | collective-permute-start | bytes 98312 | tf_op jit(solution)/shard_map/ppermute | solution.py:16
  735.5 5.8 collective-permute-start.13
Sparse Core Ops, SparseCore 0:
  10.2 67.8 all-gather.4
  159.6 21.7 reduce-scatter.4
  183.8 65.1 all-gather.2
  399.7 22.0 reduce-scatter.6
  522.5 130.9 reduce-scatter.8
  664.6 134.5 reduce-scatter.10
where the time goes:
time: 810 us; the launch traced here: 806 us
  waiting for transfers between devices  188 us (23%)
  matrix products  175 us (22%)
  local copies, waits for them, and re-layouts  147 us (18%)
  loops' own time  111 us (14%)
  other arithmetic  106 us (13%)
  starting transfers between devices  47.4 us (6%)
  between operations  22.4 us (3%)
  blocking collectives  10.9 us (1%)
    another operation x2, loops' own time, weight_term(): stacked = lax.map(advance, jnp.arange(27, dtype=jnp.int32))  106 us
    all_gather x1, waiting for transfers between devices, on_device(): second_whole = lax.all_gather(weight_second, 'space', axis=0, tiled=True)  61.3 us
    all_gather x1, waiting for transfers between devices, on_device(): segment = lax.all_gather(weight_first, 'space', axis=0, tiled=True)  59.1 us
    reduce_scatter x1, waiting for transfers between devices, on_device(): lax.psum_scatter(weight_term(ext_hidden, grad_second), 'space', scatter_d...  55.2 us
    dot_general x54, matrix products, advance(): lax.dot_general(picked, gradient, (((0,), (0,)), ((), ())), preferred_ele...  53.9 us
    ppermute x16, starting transfers between devices, passed_along(): return lax.ppermute(value, axis, pairs)  47.1 us
    scatter-add x27, other arithmetic, backward_step(): return running.at[lookup[offset]].add(contrib)  45.9 us
    scatter-add x27, other arithmetic, advance(): return current.at[lookup[offset]].add(contrib)  45.9 us
  transfers between devices with their start and end apart: 22, of which 7 were waited for; matrix products, arithmetic and copies ran while one was open for 33% of the time, Pallas kernels for 0%

commit v1 on v0

--- a/solution.py
+++ b/solution.py
@@ -1,7 +1,11 @@
+import functools
+
 import jax
 import jax.numpy as jnp
 import numpy as np
 from jax import lax
+from jax.experimental import pallas as pl
+from jax.experimental.pallas import tpu as pltpu
 from jax.sharding import PartitionSpec as P
 
 HB = 1
@@ -171,7 +175,476 @@
     return (output, features_grad, weight_first_grad, weight_second_grad)
 
 
+RULE, ROWS1, GRAD2, SUM1, BACK2, ROWS2, GRAD1, SUM2, BACK1 = range(9)
+EDGE = 6
+CELLS = EDGE**3
+HALF = 64
+MESH = pl.DeviceIdType.MESH
+
+
+def margin_tables(bricks):
+    spot = np.arange(EDGE)
+    step, local = (spot - 1) // 4 + 1, (spot - 1) % 4
+    number = 9 * step[:, None, None] + 3 * step[None, :, None] + step[None, None, :]
+    cell = 16 * local[:, None, None] + 4 * local[None, :, None] + local[None, None, :]
+    return number.reshape(-1), cell.reshape(-1)
+
+
+def low_lanes(shape):
+    return lax.broadcasted_iota(jnp.int32, shape, len(shape) - 1) < HALF
+
+
+def turned(value):
+    return pltpu.roll(value, HALF, 1)
+
+
+def halves_packed(value):
+    upper, lower = value[:64], value[64:]
+    low = low_lanes(upper.shape)
+    return (
+        jnp.where(low, upper, turned(lower)),
+        jnp.where(low, turned(upper), lower),
+    )
+
+
+def still_kernel(
+    n_s, n_c, table, features, mask, rule, first, second, cotangent,
+    output, features_grad, first_grad, second_grad,
+    rule_src, rule_buf, rows1_src, rows1_buf, rows2_src, rows2_buf,
+    grad2_src, grad2_buf, grad1_src, grad1_buf, sum1_src, sum1_buf, sum2_src, sum2_buf,
+    back2_src, back2_buf, back1_src, back1_buf,
+    pick, pick_t, order_t, wide1, wide2, margin, folded, ordered2, ordered1, running, kept_act,
+    send, recv,
+):
+    me_s, me_c = lax.axis_index("space"), lax.axis_index("chan")
+    bricks, rows = 2 * n_s, 128 * n_s
+    f32, bf16 = jnp.float32, jnp.bfloat16
+
+    def is_me(s, c):
+        return jnp.logical_and(s == me_s, c == me_c)
+
+    def remote(kind, src, buf, order, slot, s, c):
+        return pltpu.make_async_remote_copy(
+            src_ref=src, dst_ref=buf.at[slot], send_sem=send.at[kind, order],
+            recv_sem=recv.at[kind, slot], device_id=(s, c), device_id_type=MESH,
+        )
+
+    def along(kind, src_of, buf):
+        for k in range(1, n_s):
+            s = lax.rem(me_s + k, n_s)
+            yield remote(kind, src_of(s), buf, k, me_s, s, me_c), remote(
+                kind, src_of(s), buf, k, s, s, me_c
+            )
+
+    def start_along(kind, src_of, buf):
+        for out, _ in along(kind, src_of, buf):
+            out.start()
+
+    def wait_along(kind, src_of, buf):
+        for _, come in along(kind, src_of, buf):
+            come.wait_recv()
+
+    def sent_along(kind, src_of, buf):
+        for out, _ in along(kind, src_of, buf):
+            out.wait_send()
+
+    def spread(kind, src, buf, act):
+        for h in range(2):
+            for c in range(n_c):
+                s = 2 * me_c + h
+
+                @pl.when(jnp.logical_not(is_me(s, c)))
+                def _():
+                    act(remote(kind, src.at[h], buf, h * n_c + c, me_s, s, c))
+
+    def spread_wait(kind, src, buf):
+        for s in range(n_s):
+
+            @pl.when(jnp.logical_not(is_me(s, me_s // 2)))
+            def _():
+                remote(kind, src.at[0], buf, 0, s, s, me_s // 2).wait_recv()
+
+    def spread_start(kind, src, buf):
+        for h in range(2):
+
+            @pl.when(me_s == 2 * me_c + h)
+            def _():
+                buf[me_s] = src[h]
+
+        spread(kind, src, buf, lambda copy: copy.start())
+
+    def owners(kind, src, buf, act):
+        slot = (me_s % 2) * n_c + me_c
+        for s in range(n_s):
+
+            @pl.when(jnp.logical_not(is_me(s, me_s // 2)))
+            def _():
+                act(remote(kind, src.at[s], buf, s, slot, s, me_s // 2))
+
+    def owners_start(kind, src, buf):
+        @pl.when(me_s // 2 == me_c)
+        def _():
+            buf[(me_s % 2) * n_c + me_c] = src[me_s]
+
+        owners(kind, src, buf, lambda copy: copy.start())
+
+    def owners_wait(kind, src, buf):
+        for h in range(2):
+            for c in range(n_c):
+                s = 2 * me_c + h
+
+                @pl.when(jnp.logical_not(is_me(s, c)))
+                def _():
+                    remote(kind, src.at[0], buf, 0, h * n_c + c, s, c).wait_recv()
+
+    barrier = pltpu.get_barrier_semaphore()
+
+    def greet(s, c):
+        pl.semaphore_signal(barrier, inc=1, device_id=(s, c), device_id_type=MESH)
+
+    for k in range(1, n_s):
+        greet(lax.rem(me_s + k, n_s), me_c)
+    for s in range(n_s):
+
+        @pl.when(jnp.logical_not(is_me(s, me_s // 2)))
+        def _():
+            greet(s, me_s // 2)
+
+    for h in range(2):
+        for c in range(n_c):
+
+            @pl.when(jnp.logical_not(is_me(2 * me_c + h, c)))
+            def _():
+                greet(2 * me_c + h, c)
+
+    square = (128, 128)
+    diagonal = lax.broadcasted_iota(jnp.int32, square, 0) == lax.broadcasted_iota(jnp.int32, square, 1)
+    active = jnp.sum(jnp.where(diagonal, mask[...].astype(f32), 0.0), axis=1, keepdims=True)
+    masked = features[...].astype(f32) * active
+    for h, part in enumerate(halves_packed(masked)):
+        rows1_src[h] = part.astype(bf16)
+    grad2 = (cotangent[...].astype(f32) * active).astype(bf16)
+    grad2_src[...] = grad2
+    grad2_buf[me_s] = grad2
+    rule_src[...] = jnp.zeros(rule_src.shape, jnp.int32)
+    rule_src[0:2, 0:27] = rule[...]
+    place = lax.broadcasted_iota(jnp.int32, (bricks, 128), 0)
+    own_rule = jnp.where(place == 2 * me_s, rule_src[0:1, :], 0) + jnp.where(
+        place == 2 * me_s + 1, rule_src[1:2, :], 0
+    )
+    rule_src[...] = own_rule
+    rule_buf[me_s] = own_rule
+
+    greeted = n_s - 1 + n_s + 2 * n_c - 2 * jnp.where(me_s // 2 == me_c, 1, 0)
+    pl.semaphore_wait(barrier, greeted)
+    start_along(RULE, lambda s: rule_src, rule_buf)
+    spread_start(ROWS1, rows1_src, rows1_buf)
+    start_along(GRAD2, lambda s: grad2_src, grad2_buf)
+
+    lane = lax.broadcasted_iota(jnp.int32, (16, rows), 1)
+    natural = (lane % bricks) * 64 + lane // bricks
+    deep = lax.broadcasted_iota(jnp.int32, (16, rows), 0)
+
+    def order_step(r, carry):
+        at = pl.multiple_of(r * 16, 16)
+        order_t[pl.ds(at, 16), :] = jnp.where(deep + at == natural, 1.0, 0.0).astype(bf16)
+        return carry
+
+    lax.fori_loop(0, rows // 16, order_step, 0)
+
+    wait_along(RULE, lambda s: rule_src, rule_buf)
+    whole_rule = rule_buf[0]
+    for s in range(1, n_s):
+        whole_rule = whole_rule + rule_buf[s]
+    numbers, cells = margin_tables(bricks)
+    flat = lax.broadcasted_iota(jnp.int32, (bricks, rows), 1)
+    shifted = {}
+    for e in range(CELLS):
+        c = int(numbers[e])
+        if c not in shifted:
+            shifted[c] = jnp.broadcast_to(whole_rule[:, c : c + 1] * 64, (bricks, 128))
+    for e in range(CELLS):
+        target = shifted[int(numbers[e])] + int(cells[e])
+        for part in range(rows // 128):
+            pick[e * bricks : (e + 1) * bricks, part * 128 : part * 128 + 128] = jnp.where(
+                flat[:, :128] + part * 128 == target, 1.0, 0.0
+            ).astype(bf16)
+    numbers_row, cells_row = table[0:1, :], table[1:2, :]
+    depth = lax.broadcasted_iota(jnp.int32, (128, CELLS * bricks), 0)
+    chosen = jnp.where(depth == numbers_row, 1.0, 0.0).astype(bf16)
+    spots = jnp.dot(whole_rule.astype(f32).astype(bf16), chosen, preferred_element_type=f32)
+    brick_at = lax.broadcasted_iota(jnp.int32, spots.shape, 0)
+    brick_row = table[2:3, :]
+    found = jnp.sum(jnp.where(brick_at == brick_row, spots, 0.0), axis=0, keepdims=True)
+    found = found.astype(jnp.int32) * 64 + cells_row
+    tall = lax.broadcasted_iota(jnp.int32, (16, CELLS * bricks), 0)
+
+    def pick_step(r, carry):
+        at = pl.multiple_of(r * 16, 16)
+        pick_t[pl.ds(at, 16), :] = jnp.where(tall + at == found, 1.0, 0.0).astype(bf16)
+        return carry
+
+    lax.fori_loop(0, rows // 16, pick_step, 0)
+
+    slab = EDGE * EDGE * bricks
+
+    def widen(buf, wide):
+        parts = []
+        for s in range(n_s):
+            block = buf[s].astype(f32)
+            back = turned(block)
+            low = low_lanes(block.shape)
+            parts.append(jnp.where(low, block, back))
+            parts.append(jnp.where(low, back, block))
+        doubled = jnp.concatenate(parts, 0).astype(bf16)
+
+        def step(i, carry):
+            at = pl.multiple_of(i * slab, slab)
+            got = jnp.dot(pick[pl.ds(at, slab), :], doubled, preferred_element_type=f32)
+            got = got.reshape(EDGE, EDGE, bricks, 128)
+            after = jnp.concatenate([got[:, 1:], got[:, EDGE - 1 :]], 1)
+            wide[i] = jnp.where(low_lanes(got.shape), got, after).astype(bf16)
+            return carry
+
+        lax.fori_loop(0, EDGE, step, 0)
+
+    def taps(wide, i, depth_i, dy):
+        chunk = depth_i * 16 * bricks
+        near = wide[pl.ds(i, depth_i), pl.ds(dy, 4), 0:4].reshape(chunk, 128)
+        far = wide[pl.ds(i, depth_i), pl.ds(dy, 4), 2:6].reshape(chunk, 128)
+        return jnp.concatenate([near, far], 1)
+
+    def convolve(wide, weight, target, buf):
+        chunk = 16 * bricks
+
+        def step(i, carry):
+            total = jnp.zeros((chunk, 128), f32)
+            for q in range(9):
+                total = total + jnp.dot(
+                    taps(wide, i + q // 3, 1, q % 3), weight[q], preferred_element_type=f32
+                )
+            running[pl.ds(pl.multiple_of(i * chunk, chunk), chunk), :] = total.astype(bf16)
+            return carry
+
+        lax.fori_loop(0, 4, step, 0)
+        for s in range(n_s):
+            block = jnp.dot(
+                order_t[s * 128 : (s + 1) * 128, :], running[...], preferred_element_type=f32
+            ).astype(bf16)
+            target[s] = block
+        buf[me_s] = target[me_s]
+
+    def reorder(buf, ordered):
+        whole = buf[...].reshape(rows, 128)
+        for i in range(4):
+            matrix = jnp.concatenate(
+                [
+                    pick[
+                        (((i + 1) * EDGE + j + 1) * EDGE + 1) * bricks : (
+                            ((i + 1) * EDGE + j + 1) * EDGE + 5
+                        )
+                        * bricks,
+                        :,
+                    ]
+                    for j in range(4)
+                ],
+                0,
+            )
+            ordered[i * 16 * bricks : (i + 1) * 16 * bricks, :] = jnp.dot(
+                matrix, whole, preferred_element_type=f32
+            ).astype(bf16)
+
+    def transposed(ordered, weight, target):
+        margin[...] = jnp.zeros(margin.shape, f32)
+        chunk = 16 * bricks
+
+        def step(q, carry):
+            dx, dy = q // 3, q % 3
+            kernel = weight[q]
+            for i in range(4):
+                part = lax.dot_general(
+                    ordered[i * chunk : (i + 1) * chunk, :], kernel,
+                    (((1,), (1,)), ((), ())), preferred_element_type=f32,
+                )
+                near = part[:, :128].reshape(1, 4, 4, bricks, 128)
+                far = part[:, 128:].reshape(1, 4, 4, bricks, 128)
+                margin[pl.ds(i + dx, 1), pl.ds(dy, 4), 0:4] += near
+                margin[pl.ds(i + dx, 1), pl.ds(dy, 4), 2:6] += far
+            return carry
+
+        lax.fori_loop(0, 9, step, 0)
+
+        def fold(i, carry):
+            value = margin[i]
+            before = jnp.concatenate([jnp.zeros_like(value[:, :1]), value[:, : EDGE - 1]], 1)
+            both = jnp.where(low_lanes(value.shape), value, before).reshape(slab, 128)
+            folded[pl.ds(pl.multiple_of(i * slab, slab), slab), :] = (both + turned(both)).astype(bf16)
+            return carry
+
+        lax.fori_loop(0, EDGE, fold, 0)
+
+        def back(s, carry):
+            at = pl.multiple_of(s * 128, 128)
+            got = jnp.dot(pick_t[pl.ds(at, 128), :], folded[...], preferred_element_type=f32)
+            upper, lower = got[:64], got[64:]
+            target[s] = jnp.where(low_lanes(upper.shape), upper, lower).astype(bf16)
+            return carry
+
+        lax.fori_loop(0, n_s, back, 0)
+
+    def kernel_grad(wide, ordered, target):
+        def step(q, carry):
+            target[q] = lax.dot_general(
+                taps(wide, q // 3, 4, q % 3), ordered[...],
+                (((0,), (0,)), ((), ())), preferred_element_type=f32,
+            )
+            return carry
+
+        lax.fori_loop(0, 9, step, 0)
+
+    def summed(buf):
+        total = buf[0].astype(f32)
+        for s in range(1, n_s):
+            total = total + buf[s].astype(f32)
+        return total
+
+    def returned(buf):
+        sums = []
+        for h in range(2):
+            total = buf[h * n_c].astype(f32)
+            for c in range(1, n_c):
+                total = total + buf[h * n_c + c].astype(f32)
+            sums.append(total)
+        low = low_lanes(sums[0].shape)
+        return jnp.concatenate(
+            [
+                jnp.where(low, sums[0], turned(sums[1])),
+                jnp.where(low, turned(sums[0]), sums[1]),
+            ],
+            0,
+        )
+
+    spread_wait(ROWS1, rows1_src, rows1_buf)
+    widen(rows1_buf, wide1)
+    convolve(wide1, first, sum1_src, sum1_buf)
+    start_along(SUM1, lambda s: sum1_src.at[s], sum1_buf)
+    wait_along(GRAD2, lambda s: grad2_src, grad2_buf)
+    reorder(grad2_buf, ordered2)
+    transposed(ordered2, second, back2_src)
+    owners_start(BACK2, back2_src, back2_buf)
+
+    wait_along(SUM1, lambda s: sum1_src.at[s], sum1_buf)
+    act = active * summed(sum1_buf)
+    hidden = act * jax.nn.sigmoid(act)
+    for h, part in enumerate(halves_packed(hidden)):
+        rows2_src[h] = part.astype(bf16)
+    spread_start(ROWS2, rows2_src, rows2_buf)
+    kept_act[...] = act
+
+    owners_wait(BACK2, back2_src, back2_buf)
+    act = kept_act[...]
+    gate = jax.nn.sigmoid(act)
+    grad1 = (active * returned(back2_buf) * gate * (1.0 + act * (1.0 - gate))).astype(bf16)
+    grad1_src[...] = grad1
+    grad1_buf[me_s] = grad1
+    start_along(GRAD1, lambda s: grad1_src, grad1_buf)
+
+    spread_wait(ROWS2, rows2_src, rows2_buf)
+    widen(rows2_buf, wide2)
+    convolve(wide2, second, sum2_src, sum2_buf)
+    start_along(SUM2, lambda s: sum2_src.at[s], sum2_buf)
+    wait_along(GRAD1, lambda s: grad1_src, grad1_buf)
+    reorder(grad1_buf, ordered1)
+    transposed(ordered1, first, back1_src)
+    owners_start(BACK1, back1_src, back1_buf)
+
+    kernel_grad(wide2, ordered2, second_grad)
+    kernel_grad(wide1, ordered1, first_grad)
+
+    wait_along(SUM2, lambda s: sum2_src.at[s], sum2_buf)
+    output[...] = active * summed(sum2_buf)
+    owners_wait(BACK1, back1_src, back1_buf)
+    features_grad[...] = active * returned(back1_buf)
+
+    sent_along(RULE, lambda s: rule_src, rule_buf)
+    sent_along(GRAD2, lambda s: grad2_src, grad2_buf)
+    sent_along(GRAD1, lambda s: grad1_src, grad1_buf)
+    sent_along(SUM1, lambda s: sum1_src.at[s], sum1_buf)
+    sent_along(SUM2, lambda s: sum2_src.at[s], sum2_buf)
+    spread(ROWS1, rows1_src, rows1_buf, lambda copy: copy.wait_send())
+    spread(ROWS2, rows2_src, rows2_buf, lambda copy: copy.wait_send())
+    owners(BACK2, back2_src, back2_buf, lambda copy: copy.wait_send())
+    owners(BACK1, back1_src, back1_buf, lambda copy: copy.wait_send())
+
+
+def still_weights(n_s, n_c, features, mask, rulebook, weight_first, weight_second, cotangent):
+    bricks, rows = 2 * n_s, 128 * n_s
+    numbers, cells = margin_tables(bricks)
+    table = np.zeros((8, CELLS * bricks), np.int32)
+    table[0] = np.repeat(numbers, bricks)
+    table[1] = np.repeat(cells, bricks)
+    table[2] = np.tile(np.arange(bricks), CELLS)
+    f32, bf16 = jnp.float32, jnp.bfloat16
+
+    def stacked(weight):
+        moved = jnp.transpose(weight, (1, 0, 2)).reshape(9, 3 * 64, 128)
+        return jnp.pad(moved, ((0, 0), (0, 64), (0, 0)))
+
+    def buffers(shape, kind, sources=None):
+        return [pltpu.VMEM(sources or shape, kind), pltpu.VMEM(shape, kind)]
+
+    wide = (EDGE, EDGE, EDGE, bricks, 128)
+    packed, square = (n_s, 64, 128), (n_s, 128, 128)
+    scratch = (
+        buffers((n_s, bricks, 128), jnp.int32, (bricks, 128))
+        + buffers(packed, bf16, (2, 64, 128)) * 2
+        + buffers(square, bf16, (128, 128)) * 2
+        + buffers(square, bf16) * 2
+        + buffers(packed, bf16) * 2
+        + [
+            pltpu.VMEM((CELLS * bricks, rows), bf16),
+            pltpu.VMEM((rows, CELLS * bricks), bf16),
+            pltpu.VMEM((rows, rows), bf16),
+            pltpu.VMEM(wide, bf16),
+            pltpu.VMEM(wide, bf16),
+            pltpu.VMEM(wide, f32),
+            pltpu.VMEM((CELLS * bricks, 128), bf16),
+            pltpu.VMEM((rows, 128), bf16),
+            pltpu.VMEM((rows, 128), bf16),
+            pltpu.VMEM((rows, 128), bf16),
+            pltpu.VMEM((128, 128), f32),
+            pltpu.SemaphoreType.DMA((9, max(n_s, 2 * n_c))),
+            pltpu.SemaphoreType.DMA((9, max(n_s, 2 * n_c))),
+        ]
+    )
+    output, features_grad, first_grad, second_grad = pl.pallas_call(
+        functools.partial(still_kernel, n_s, n_c),
+        out_shape=[jax.ShapeDtypeStruct((128, 128), f32)] * 2
+        + [jax.ShapeDtypeStruct((9, 256, 128), f32)] * 2,
+        in_specs=[pl.BlockSpec(memory_space=pltpu.VMEM)] * 7,
+        out_specs=[pl.BlockSpec(memory_space=pltpu.VMEM)] * 4,
+        scratch_shapes=scratch,
+        compiler_params=pltpu.CompilerParams(
+            collective_id=0, has_side_effects=True, vmem_limit_bytes=56 * 2**20
+        ),
+    )(
+        table, features, mask.reshape(1, 128), rulebook,
+        stacked(weight_first), stacked(weight_second), cotangent,
+    )
+
+    def unstacked(grad):
+        return jnp.transpose(grad[:, : 3 * 64].reshape(27, 64, 128), (1, 0, 2))
+
+    return (
+        output.astype(bf16), features_grad.astype(bf16), unstacked(first_grad), unstacked(second_grad),
+    )
+
+
 def solution(mesh):
+    n_space, n_chan = mesh.shape["space"], mesh.shape["chan"]
+    body = on_device
+    if n_space == 2 * n_chan and n_space <= 8:
+        body = functools.partial(still_weights, n_space, n_chan)
     placed = (
         P("space", "chan"),
         P("space"),
@@ -181,7 +654,7 @@
         P("space", "chan"),
     )
     return jax.shard_map(
-        on_device,
+        body,
         mesh=mesh,
         in_specs=placed,
         out_specs=(

time: 810 us -> 75.9 us (0.09)
  waiting for transfers between devices: 188 us -> 0 us
  matrix products: 175 us -> 0 us
  local copies, waits for them, and re-layouts: 147 us -> 5.93 us
  loops' own time: 111 us -> 0 us
  other arithmetic: 106 us -> 3.01 us
  Pallas kernels: 0 us -> 64.9 us
  starting transfers between devices: 47.4 us -> 0 us
  between operations: 22.4 us -> 0.66 us
  blocking collectives: 10.9 us -> 0 us
    dot_general x162 -> x0, matrix products: 175 us -> none  [the longest x54 53.9 us: advance(): lax.dot_general(picked, gradient, (((0,), (0,)), ((), ())), preferred_ele...]
    all_gather x2 -> x0, waiting for transfers between devices: 120 us -> none  [the longest x1 61.3 us: on_device(): second_whole = lax.all_gather(weight_second, 'space', axis=0, tiled=True)]
    another operation x6 -> x0, loops' own time: 111 us -> none  [the longest x2 106 us: weight_term(): stacked = lax.map(advance, jnp.arange(27, dtype=jnp.int32))]
    scatter-add x62 -> x0, other arithmetic: 96.9 us -> none  [the longest x27 45.9 us: backward_step(): return running.at[lookup[offset]].add(contrib)]
    gather x109 -> x0, local copies, waits for them, and re-layouts: 94.9 us -> none  [the longest x54 45.8 us: advance(): picked = jnp.take(extended, lookup[offset], axis=0)]
    pallas_call x0 -> x1, Pallas kernels: none -> 64.9 us  [still_weights(): pl.pallas_call(functools.partial(still_kernel, n_s, n_c), out_shape=[jax....]
    reduce_scatter x4 -> x0, waiting for transfers between devices: 55.2 us -> none  [the longest x1 55.2 us: on_device(): lax.psum_scatter(weight_term(ext_hidden, grad_second), 'space', scatter_d...]
    ppermute x16 -> x0, starting transfers between devices: 47.1 us -> none  [passed_along(): return lax.ppermute(value, axis, pairs)]
  transfers between devices with their start and end apart: 22 -> 0, of which waited for: 7 -> 0; matrix products, arithmetic and copies ran while one was open for 33% -> 0% of each run, Pallas kernels for 0% -> 0%
where the time goes in v1:
time: 75.9 us; the launch traced here: 74.5 us
  Pallas kernels  64.9 us (86%)
  local copies, waits for them, and re-layouts  5.93 us (8%)
  other arithmetic  3.01 us (4%)
    pallas_call x1, Pallas kernels, still_weights(): pl.pallas_call(functools.partial(still_kernel, n_s, n_c), out_shape=[jax....  64.9 us
    slice x2, local copies, waits for them, and re-layouts, unstacked(): return jnp.transpose(grad[:, :3 * 64].reshape(27, 64, 128), (1, 0, 2))  3.11 us
    pad x2, local copies, waits for them, and re-layouts, stacked(): return jnp.pad(moved, ((0, 0), (0, 64), (0, 0)))  2.82 us
    convert_element_type x1, other arithmetic, still_weights(): output.astype(bf16)  1.55 us

profile of v1, /device:TPU:0, one launch (start us, length us, event | category | flops | bytes accessed | tf_op | source)
XLA Modules:
  0.0 74.5 jit_solution(9465719913165321008)
XLA Ops:
  0.6 0.0 copy-start.1
  0.6 1.9 %pad.7.first = bf16[9,256,128]{2,1,0:T(8,128)(2,1)} pad(bf16[9,192,128]{2,1,0:T(8,128)(2,1)} %bitcast.15, bf16[]{:T(256)} %constant.4.clone.1), padding=0_0x0_64x0_0 | pad | bytes 1032194 | tf_op jit(solution)/shard_map/jit(_pad)/pad | solution.py:591
  2.6 0.0 copy-done.1
  2.6 0.9 %pad.8.second = bf16[9,256,128]{2,1,0:T(8,128)(2,1)} pad(bf16[9,192,128]{2,1,0:T(8,128)(2,1)S(1)} %bitcast.16, bf16[]{:T(256)} %constant.4.clone.1), padding=0_0x0_64x0_0 | pad | bytes 1032194 | tf_op jit(solution)/shard_map/jit(_pad)/pad | solution.py:591
  3.5 64.9 %shard_map.102 = (f32[128,128]{1,0:T(8,128)}, f32[128,128]{1,0:T(8,128)}, f32[9,256,128]{2,1,0:T(8,128)}, f32[9,256,128]{2,1,0:T(8,128)}) custom-call(s32[8,3456]{1,0:T(8,128)} %constant.5.clone.table, bf16[128,128]{1,0:T(8,128)(2,1)} %features.1, s32[1,128]{1,0:T(1,128)} %bitcast.17, s32[2,27]{1,0:T(2,128)} %rule.1, bf16[9,256,128]{2,1,0:T(8,128)(2,1)} %pad.7.first, ...), custom_call_target="tpu_custom_call" | custom-call | tf_op jit(solution)/shard_map/pallas_call | solution.py:620
  68.4 0.0 copy-start
  68.4 1.6 %convert_element_type.9 = bf16[128,128]{1,0:T(8,128)(2,1)} convert(f32[128,128]{1,0:T(8,128)} %get-tuple-element.8) | non-fusion elementwise | flops 16384 | bytes 98304 | tf_op jit(solution)/shard_map/convert_element_type | solution.py:639
  70.0 1.5 %convert_element_type.10 = bf16[128,128]{1,0:T(8,128)(2,1)} convert(f32[128,128]{1,0:T(8,128)} %get-tuple-element.9) | non-fusion elementwise | flops 16384 | bytes 98304 | tf_op jit(solution)/shard_map/convert_element_type | solution.py:639
  71.4 2.1 %slice.6 = f32[9,192,128]{2,1,0:T(8,128)} slice(f32[9,256,128]{2,1,0:T(8,128)} %get-tuple-element.10), slice={[0:9], [0:192], [0:128]} | slice | bytes 1769472 | tf_op jit(solution)/shard_map/slice | solution.py:636
  73.6 0.0 copy-done
  73.6 1.0 %slice.7 = f32[9,192,128]{2,1,0:T(8,128)} slice(f32[9,256,128]{2,1,0:T(8,128)S(1)} %copy-done), slice={[0:9], [0:192], [0:128]} | slice | bytes 1769472 | tf_op jit(solution)/shard_map/slice | solution.py:636
Async XLA Ops:
  0.6 2.0 %copy-start.1 = (bf16[64,27,128]{2,0,1:T(8,128)(2,1)S(1)}, bf16[64,27,128]{2,0,1:T(8,128)(2,1)}, u32[]{:S(2)}) copy-start(bf16[64,27,128]{2,0,1:T(8,128)(2,1)} %param.11) | copy-start | bytes 1327108
  68.4 5.2 %copy-start = (f32[9,256,128]{2,1,0:T(8,128)S(1)}, f32[9,256,128]{2,1,0:T(8,128)}, u32[]{:S(2)}) copy-start(f32[9,256,128]{2,1,0:T(8,128)} %get-tuple-element.11) | copy-start | bytes 3538948

commit v2 on v1

--- a/solution.py
+++ b/solution.py
@@ -177,17 +177,23 @@
 
 RULE, ROWS1, GRAD2, SUM1, BACK2, ROWS2, GRAD1, SUM2, BACK1 = range(9)
 EDGE = 6
-CELLS = EDGE**3
 HALF = 64
 MESH = pl.DeviceIdType.MESH
 
 
-def margin_tables(bricks):
-    spot = np.arange(EDGE)
-    step, local = (spot - 1) // 4 + 1, (spot - 1) % 4
-    number = 9 * step[:, None, None] + 3 * step[None, :, None] + step[None, None, :]
-    cell = 16 * local[:, None, None] + 4 * local[None, :, None] + local[None, None, :]
-    return number.reshape(-1), cell.reshape(-1)
+def brick_offsets():
+    targets, sources = (slice(0, 1), slice(1, 5), slice(5, 6)), (slice(4, 5), slice(1, 5), slice(1, 2))
+    counts = {16: 0, 4: 0, 1: 0}
+    found = []
+    for c in range(27):
+        moves = (c // 9, c // 3 % 3, c % 3)
+        cells = 4 ** moves.count(1)
+        if c != 13:
+            found.append(
+                (c, cells, counts[cells], tuple(targets[m] for m in moves), tuple(sources[m] for m in moves))
+            )
+            counts[cells] += 1
+    return found
 
 
 def low_lanes(shape):
@@ -208,12 +214,13 @@
 
 
 def still_kernel(
-    n_s, n_c, table, features, mask, rule, first, second, cotangent,
+    n_s, n_c, features, mask, rule, first, second, cotangent,
     output, features_grad, first_grad, second_grad,
     rule_src, rule_buf, rows1_src, rows1_buf, rows2_src, rows2_buf,
     grad2_src, grad2_buf, grad1_src, grad1_buf, sum1_src, sum1_buf, sum2_src, sum2_buf,
     back2_src, back2_buf, back1_src, back1_buf,
-    pick, pick_t, order_t, wide1, wide2, margin, folded, ordered2, ordered1, running, kept_act,
+    faces, edges, corners, order, order_t, raw, wide1, wide2, margin,
+    ordered2, ordered1, flipped2, flipped1, running, kept_act, first_stack, second_stack,
     send, recv,
 ):
     me_s, me_c = lax.axis_index("space"), lax.axis_index("chan")
@@ -348,43 +355,31 @@
     def order_step(r, carry):
         at = pl.multiple_of(r * 16, 16)
         order_t[pl.ds(at, 16), :] = jnp.where(deep + at == natural, 1.0, 0.0).astype(bf16)
+        order[pl.ds(at, 16), :] = jnp.where(deep * 64 + r == lane, 1.0, 0.0).astype(bf16)
         return carry
 
     lax.fori_loop(0, rows // 16, order_step, 0)
+    for weight, stack in ((first, first_stack), (second, second_stack)):
+        for q in range(9):
+            stack[q, 0:192, :] = weight[3 * q : 3 * q + 3].reshape(192, 128)
+            stack[q, 192:256, :] = jnp.zeros((64, 128), bf16)
 
     wait_along(RULE, lambda s: rule_src, rule_buf)
     whole_rule = rule_buf[0]
     for s in range(1, n_s):
         whole_rule = whole_rule + rule_buf[s]
-    numbers, cells = margin_tables(bricks)
-    flat = lax.broadcasted_iota(jnp.int32, (bricks, rows), 1)
-    shifted = {}
-    for e in range(CELLS):
-        c = int(numbers[e])
-        if c not in shifted:
-            shifted[c] = jnp.broadcast_to(whole_rule[:, c : c + 1] * 64, (bricks, 128))
-    for e in range(CELLS):
-        target = shifted[int(numbers[e])] + int(cells[e])
-        for part in range(rows // 128):
-            pick[e * bricks : (e + 1) * bricks, part * 128 : part * 128 + 128] = jnp.where(
-                flat[:, :128] + part * 128 == target, 1.0, 0.0
-            ).astype(bf16)
-    numbers_row, cells_row = table[0:1, :], table[1:2, :]
-    depth = lax.broadcasted_iota(jnp.int32, (128, CELLS * bricks), 0)
-    chosen = jnp.where(depth == numbers_row, 1.0, 0.0).astype(bf16)
-    spots = jnp.dot(whole_rule.astype(f32).astype(bf16), chosen, preferred_element_type=f32)
-    brick_at = lax.broadcasted_iota(jnp.int32, spots.shape, 0)
-    brick_row = table[2:3, :]
-    found = jnp.sum(jnp.where(brick_at == brick_row, spots, 0.0), axis=0, keepdims=True)
-    found = found.astype(jnp.int32) * 64 + cells_row
-    tall = lax.broadcasted_iota(jnp.int32, (16, CELLS * bricks), 0)
-
-    def pick_step(r, carry):
-        at = pl.multiple_of(r * 16, 16)
-        pick_t[pl.ds(at, 16), :] = jnp.where(tall + at == found, 1.0, 0.0).astype(bf16)
-        return carry
-
-    lax.fori_loop(0, rows // 16, pick_step, 0)
+    whole_rule = jnp.where(whole_rule < 0, -4096, whole_rule)
+    which = {16: faces, 4: edges, 1: corners}
+    for c, cells, at, _, _ in brick_offsets():
+        fed = jnp.broadcast_to(whole_rule[:, c : c + 1], (bricks, 128))
+        span = cells * bricks
+        for cell in range(cells):
+            for part in range(0, span, 128):
+                width = min(128, span - part)
+                hit = lane[:, :128] + (part - cell * bricks) == fed
+                which[cells][at, cell * bricks : (cell + 1) * bricks, part : part + width] = (
+                    jnp.where(hit, 1.0, 0.0).astype(bf16)[:, :width]
+                )
 
     slab = EDGE * EDGE * bricks
 
@@ -398,10 +393,16 @@
             parts.append(jnp.where(low, back, block))
         doubled = jnp.concatenate(parts, 0).astype(bf16)
 
+        for i in range(4):
+            got = jnp.dot(order[i * 256 : (i + 1) * 256, :], doubled, preferred_element_type=f32)
+            raw[i + 1, 1:5, 1:5] = got.reshape(4, 4, bricks, 128).astype(bf16)
+        for c, cells, at, target, source in brick_offsets():
+            value = raw[source].reshape(cells * bricks, 128)
+            got = jnp.dot(which[cells][at], value, preferred_element_type=f32)
+            raw[target] = got.astype(bf16).reshape(raw[target].shape)
+
         def step(i, carry):
-            at = pl.multiple_of(i * slab, slab)
-            got = jnp.dot(pick[pl.ds(at, slab), :], doubled, preferred_element_type=f32)
-            got = got.reshape(EDGE, EDGE, bricks, 128)
+            got = raw[i].astype(f32)
             after = jnp.concatenate([got[:, 1:], got[:, EDGE - 1 :]], 1)
             wide[i] = jnp.where(low_lanes(got.shape), got, after).astype(bf16)
             return carry
@@ -434,25 +435,12 @@
             target[s] = block
         buf[me_s] = target[me_s]
 
-    def reorder(buf, ordered):
+    def reorder(buf, ordered, flipped):
         whole = buf[...].reshape(rows, 128)
         for i in range(4):
-            matrix = jnp.concatenate(
-                [
-                    pick[
-                        (((i + 1) * EDGE + j + 1) * EDGE + 1) * bricks : (
-                            ((i + 1) * EDGE + j + 1) * EDGE + 5
-                        )
-                        * bricks,
-                        :,
-                    ]
-                    for j in range(4)
-                ],
-                0,
-            )
-            ordered[i * 16 * bricks : (i + 1) * 16 * bricks, :] = jnp.dot(
-                matrix, whole, preferred_element_type=f32
-            ).astype(bf16)
+            got = jnp.dot(order[i * 256 : (i + 1) * 256, :], whole, preferred_element_type=f32)
+            ordered[i * 256 : (i + 1) * 256, :] = got.astype(bf16)
+            flipped[:, i * 256 : (i + 1) * 256] = got.T.astype(bf16)
 
     def transposed(ordered, weight, target):
         margin[...] = jnp.zeros(margin.shape, f32)
@@ -478,26 +466,33 @@
             value = margin[i]
             before = jnp.concatenate([jnp.zeros_like(value[:, :1]), value[:, : EDGE - 1]], 1)
             both = jnp.where(low_lanes(value.shape), value, before).reshape(slab, 128)
-            folded[pl.ds(pl.multiple_of(i * slab, slab), slab), :] = (both + turned(both)).astype(bf16)
+            margin[i] = (both + turned(both)).reshape(value.shape)
             return carry
 
         lax.fori_loop(0, EDGE, fold, 0)
+        for c, cells, at, source, owner in brick_offsets():
+            value = margin[source].reshape(cells * bricks, 128)
+            coarse = value.astype(bf16).astype(f32)
+            split = jnp.where(low_lanes(value.shape), coarse, value - coarse).astype(bf16)
+            got = lax.dot_general(
+                which[cells][at], split, (((0,), (0,)), ((), ())), preferred_element_type=f32
+            )
+            margin[owner] += (got + turned(got)).reshape(margin[owner].shape)
+        running[...] = margin[1:5, 1:5, 1:5].reshape(rows, 128).astype(bf16)
 
         def back(s, carry):
             at = pl.multiple_of(s * 128, 128)
-            got = jnp.dot(pick_t[pl.ds(at, 128), :], folded[...], preferred_element_type=f32)
+            got = jnp.dot(order_t[pl.ds(at, 128), :], running[...], preferred_element_type=f32)
             upper, lower = got[:64], got[64:]
             target[s] = jnp.where(low_lanes(upper.shape), upper, lower).astype(bf16)
             return carry
 
         lax.fori_loop(0, n_s, back, 0)
 
-    def kernel_grad(wide, ordered, target):
+    def kernel_grad(wide, flipped, target):
         def step(q, carry):
-            target[q] = lax.dot_general(
-                taps(wide, q // 3, 4, q % 3), ordered[...],
-                (((0,), (0,)), ((), ())), preferred_element_type=f32,
-            )
+            got = jnp.dot(flipped[...], taps(wide, q // 3, 4, q % 3), preferred_element_type=f32)
+            target[pl.ds(3 * q, 3)] = got.T[:192].reshape(3, 64, 128)
             return carry
 
         lax.fori_loop(0, 9, step, 0)
@@ -526,11 +521,11 @@
 
     spread_wait(ROWS1, rows1_src, rows1_buf)
     widen(rows1_buf, wide1)
-    convolve(wide1, first, sum1_src, sum1_buf)
+    convolve(wide1, first_stack, sum1_src, sum1_buf)
     start_along(SUM1, lambda s: sum1_src.at[s], sum1_buf)
     wait_along(GRAD2, lambda s: grad2_src, grad2_buf)
-    reorder(grad2_buf, ordered2)
-    transposed(ordered2, second, back2_src)
+    reorder(grad2_buf, ordered2, flipped2)
+    transposed(ordered2, second_stack, back2_src)
     owners_start(BACK2, back2_src, back2_buf)
 
     wait_along(SUM1, lambda s: sum1_src.at[s], sum1_buf)
@@ -551,20 +546,20 @@
 
     spread_wait(ROWS2, rows2_src, rows2_buf)
     widen(rows2_buf, wide2)
-    convolve(wide2, second, sum2_src, sum2_buf)
+    convolve(wide2, second_stack, sum2_src, sum2_buf)
     start_along(SUM2, lambda s: sum2_src.at[s], sum2_buf)
     wait_along(GRAD1, lambda s: grad1_src, grad1_buf)
-    reorder(grad1_buf, ordered1)
-    transposed(ordered1, first, back1_src)
+    reorder(grad1_buf, ordered1, flipped1)
+    transposed(ordered1, first_stack, back1_src)
     owners_start(BACK1, back1_src, back1_buf)
 
-    kernel_grad(wide2, ordered2, second_grad)
-    kernel_grad(wide1, ordered1, first_grad)
+    kernel_grad(wide2, flipped2, second_grad)
+    kernel_grad(wide1, flipped1, first_grad)
 
     wait_along(SUM2, lambda s: sum2_src.at[s], sum2_buf)
-    output[...] = active * summed(sum2_buf)
+    output[...] = (active * summed(sum2_buf)).astype(bf16)
     owners_wait(BACK1, back1_src, back1_buf)
-    features_grad[...] = active * returned(back1_buf)
+    features_grad[...] = (active * returned(back1_buf)).astype(bf16)
 
     sent_along(RULE, lambda s: rule_src, rule_buf)
     sent_along(GRAD2, lambda s: grad2_src, grad2_buf)
@@ -579,16 +574,10 @@
 
 def still_weights(n_s, n_c, features, mask, rulebook, weight_first, weight_second, cotangent):
     bricks, rows = 2 * n_s, 128 * n_s
-    numbers, cells = margin_tables(bricks)
-    table = np.zeros((8, CELLS * bricks), np.int32)
-    table[0] = np.repeat(numbers, bricks)
-    table[1] = np.repeat(cells, bricks)
-    table[2] = np.tile(np.arange(bricks), CELLS)
     f32, bf16 = jnp.float32, jnp.bfloat16
 
     def stacked(weight):
-        moved = jnp.transpose(weight, (1, 0, 2)).reshape(9, 3 * 64, 128)
-        return jnp.pad(moved, ((0, 0), (0, 64), (0, 0)))
+        return jnp.transpose(weight, (1, 0, 2))
 
     def buffers(shape, kind, sources=None):
         return [pltpu.VMEM(sources or shape, kind), pltpu.VMEM(shape, kind)]
@@ -602,48 +591,54 @@
         + buffers(square, bf16) * 2
         + buffers(packed, bf16) * 2
         + [
-            pltpu.VMEM((CELLS * bricks, rows), bf16),
-            pltpu.VMEM((rows, CELLS * bricks), bf16),
+            pltpu.VMEM((6, 256, 256), bf16),
+            pltpu.VMEM((12, 64, 64), bf16),
+            pltpu.VMEM((8, 16, 16), bf16),
+            pltpu.VMEM((rows, rows), bf16),
             pltpu.VMEM((rows, rows), bf16),
             pltpu.VMEM(wide, bf16),
             pltpu.VMEM(wide, bf16),
+            pltpu.VMEM(wide, bf16),
             pltpu.VMEM(wide, f32),
-            pltpu.VMEM((CELLS * bricks, 128), bf16),
             pltpu.VMEM((rows, 128), bf16),
             pltpu.VMEM((rows, 128), bf16),
+            pltpu.VMEM((128, rows), bf16),
+            pltpu.VMEM((128, rows), bf16),
             pltpu.VMEM((rows, 128), bf16),
             pltpu.VMEM((128, 128), f32),
+            pltpu.VMEM((9, 256, 128), bf16),
+            pltpu.VMEM((9, 256, 128), bf16),
             pltpu.SemaphoreType.DMA((9, max(n_s, 2 * n_c))),
             pltpu.SemaphoreType.DMA((9, max(n_s, 2 * n_c))),
         ]
     )
     output, features_grad, first_grad, second_grad = pl.pallas_call(
         functools.partial(still_kernel, n_s, n_c),
-        out_shape=[jax.ShapeDtypeStruct((128, 128), f32)] * 2
-        + [jax.ShapeDtypeStruct((9, 256, 128), f32)] * 2,
-        in_specs=[pl.BlockSpec(memory_space=pltpu.VMEM)] * 7,
+        out_shape=[jax.ShapeDtypeStruct((128, 128), bf16)] * 2
+        + [jax.ShapeDtypeStruct((27, 64, 128), f32)] * 2,
+        in_specs=[pl.BlockSpec(memory_space=pltpu.VMEM)] * 6,
         out_specs=[pl.BlockSpec(memory_space=pltpu.VMEM)] * 4,
         scratch_shapes=scratch,
         compiler_params=pltpu.CompilerParams(
-            collective_id=0, has_side_effects=True, vmem_limit_bytes=56 * 2**20
+            collective_id=0, has_side_effects=True, vmem_limit_bytes=48 * 2**20
         ),
     )(
-        table, features, mask.reshape(1, 128), rulebook,
+        features, mask.reshape(1, 128), rulebook,
         stacked(weight_first), stacked(weight_second), cotangent,
     )
 
     def unstacked(grad):
-        return jnp.transpose(grad[:, : 3 * 64].reshape(27, 64, 128), (1, 0, 2))
+        return jnp.transpose(grad, (1, 0, 2))
 
     return (
-        output.astype(bf16), features_grad.astype(bf16), unstacked(first_grad), unstacked(second_grad),
+        output, features_grad, unstacked(first_grad), unstacked(second_grad),
     )
 
 
 def solution(mesh):
     n_space, n_chan = mesh.shape["space"], mesh.shape["chan"]
     body = on_device
-    if n_space == 2 * n_chan and n_space <= 8:
+    if n_space == 8 and n_chan == 4:
         body = functools.partial(still_weights, n_space, n_chan)
     placed = (
         P("space", "chan"),

time: 75.9 us -> 66.1 us (0.87)
  Pallas kernels: 64.9 us -> 57.1 us
  other arithmetic: 3.01 us -> 0 us
  local copies, waits for them, and re-layouts: 5.93 us -> 7.26 us
    pallas_call x1, Pallas kernels: 64.9 us -> 57.1 us  [still_weights(): pl.pallas_call(functools.partial(still_kernel, n_s, n_c), out_shape=[jax....]
    unnamed x4 -> x16, local copies, waits for them, and re-layouts: 0.01 us -> 7.26 us
    slice x2 -> x0, local copies, waits for them, and re-layouts: 3.11 us -> none  [unstacked(): return jnp.transpose(grad[:, :3 * 64].reshape(27, 64, 128), (1, 0, 2))]
    convert_element_type x2 -> x0, other arithmetic: 3.01 us -> none  [the longest x1 1.55 us: still_weights(): output.astype(bf16)]
    pad x2 -> x0, local copies, waits for them, and re-layouts: 2.82 us -> none  [stacked(): return jnp.pad(moved, ((0, 0), (0, 64), (0, 0)))]
where the time goes in v2:
time: 66.1 us; the launch traced here: 65 us
  Pallas kernels  57.1 us (86%)
  local copies, waits for them, and re-layouts  7.26 us (11%)
    pallas_call x1, Pallas kernels, still_weights(): pl.pallas_call(functools.partial(still_kernel, n_s, n_c), out_shape=[jax....  57.1 us
    unnamed x16, local copies, waits for them, and re-layouts  7.26 us

profile of v2, /device:TPU:0, one launch (start us, length us, event | category | flops | bytes accessed | tf_op | source)
XLA Modules:
  0.0 65.0 jit_solution(13386098758465759240)
XLA Ops:
  0.6 0.0 copy-start.4
  0.6 0.0 copy-start.5
  0.7 0.7 %copy-done.4 = s32[2,27]{1,0:T(2,128)S(1)} copy-done((s32[2,27]{1,0:T(2,128)S(1)}, s32[2,27]{1,0:T(2,128)}, u32[]{:S(2)}) %copy-start.4) | copy-done | bytes 240
  1.3 0.0 copy-done.5
  1.3 0.0 copy-start
  1.3 1.0 %copy-done = bf16[64,27,128]{2,0,1:T(8,128)(2,1)S(1)} copy-done((bf16[64,27,128]{2,0,1:T(8,128)(2,1)S(1)}, bf16[64,27,128]{2,0,1:T(8,128)(2,1)}, u32[]{:S(2)}) %copy-start) | copy-done | bytes 442392
  2.3 0.0 copy-start.1
  2.3 1.0 %copy-done.1 = bf16[64,27,128]{2,0,1:T(8,128)(2,1)S(1)} copy-done((bf16[64,27,128]{2,0,1:T(8,128)(2,1)S(1)}, bf16[64,27,128]{2,0,1:T(8,128)(2,1)}, u32[]{:S(2)}) %copy-start.1) | copy-done | bytes 442392
  3.3 0.0 copy-start.2
  3.3 0.8 %copy-done.2 = bf16[128,128]{1,0:T(8,128)(2,1)S(1)} copy-done((bf16[128,128]{1,0:T(8,128)(2,1)S(1)}, bf16[128,128]{1,0:T(8,128)(2,1)}, u32[]{:S(2)}) %copy-start.2) | copy-done | bytes 32792
  4.1 0.0 copy-start.3
  4.1 0.8 %copy-done.3 = bf16[128,128]{1,0:T(8,128)(2,1)S(1)} copy-done((bf16[128,128]{1,0:T(8,128)(2,1)S(1)}, bf16[128,128]{1,0:T(8,128)(2,1)}, u32[]{:S(2)}) %copy-start.3) | copy-done | bytes 32792
  4.9 57.1 %shard_map.93 = (bf16[128,128]{1,0:T(8,128)(2,1)S(1)}, bf16[128,128]{1,0:T(8,128)(2,1)S(1)}, f32[27,64,128]{2,1,0:T(8,128)S(1)}, f32[27,64,128]{2,1,0:T(8,128)S(1)}) custom-call(bf16[128,128]{1,0:T(8,128)(2,1)S(1)} %copy-done.2, s32[1,128]{1,0:T(1,128)S(1)} %bitcast.9, s32[2,27]{1,0:T(2,128)S(1)} %copy-done.4, bf16[27,64,128]{2,1,0:T(8,128)(2,1)S(1)} %bitcast.7, ...), custom_call_target="tpu_custom_call" | custom-call | tf_op jit(solution)/shard_map/pallas_call | solution.py:615
  62.0 0.6 copy.14
  62.6 0.6 copy.15
  63.2 0.9 %copy.16 = f32[64,27,128]{2,0,1:T(8,128)} copy(f32[64,27,128]{2,0,1:T(8,128)S(1)} %bitcast.6) | data formatting | bytes 1769472
  64.1 0.9 %copy.17 = f32[64,27,128]{2,0,1:T(8,128)} copy(f32[64,27,128]{2,0,1:T(8,128)S(1)} %bitcast.5) | data formatting | bytes 1769472
Async XLA Ops:
  0.6 0.7 %copy-start.4 = (s32[2,27]{1,0:T(2,128)S(1)}, s32[2,27]{1,0:T(2,128)}, u32[]{:S(2)}) copy-start(s32[2,27]{1,0:T(2,128)} %rule.1) | copy-start | bytes 652
  0.6 0.7 %copy-start.5 = (s32[128]{0:T(128)S(1)}, s32[128]{0:T(128)}, u32[]{:S(2)}) copy-start(s32[128]{0:T(128)} %param.7) | copy-start | bytes 1540
  1.3 1.0 %copy-start = (bf16[64,27,128]{2,0,1:T(8,128)(2,1)S(1)}, bf16[64,27,128]{2,0,1:T(8,128)(2,1)}, u32[]{:S(2)}) copy-start(bf16[64,27,128]{2,0,1:T(8,128)(2,1)} %param.9) | copy-start | bytes 1327108
  2.3 1.0 %copy-start.1 = (bf16[64,27,128]{2,0,1:T(8,128)(2,1)S(1)}, bf16[64,27,128]{2,0,1:T(8,128)(2,1)}, u32[]{:S(2)}) copy-start(bf16[64,27,128]{2,0,1:T(8,128)(2,1)} %param.10) | copy-start | bytes 1327108
  3.3 0.8 %copy-start.2 = (bf16[128,128]{1,0:T(8,128)(2,1)S(1)}, bf16[128,128]{1,0:T(8,128)(2,1)}, u32[]{:S(2)}) copy-start(bf16[128,128]{1,0:T(8,128)(2,1)} %features.1) | copy-start | bytes 98308
  4.1 0.8 %copy-start.3 = (bf16[128,128]{1,0:T(8,128)(2,1)S(1)}, bf16[128,128]{1,0:T(8,128)(2,1)}, u32[]{:S(2)}) copy-start(bf16[128,128]{1,0:T(8,128)(2,1)} %cotangent.1) | copy-start | bytes 98308

commit v3 on v2

--- a/solution.py
+++ b/solution.py
@@ -175,7 +175,7 @@
     return (output, features_grad, weight_first_grad, weight_second_grad)
 
 
-RULE, ROWS1, GRAD2, SUM1, BACK2, ROWS2, GRAD1, SUM2, BACK1 = range(9)
+RULE, ROWS1, GRAD2, SUM1, PART2, BACK2, ROWS2, GRAD1, SUM2, PART1, BACK1 = range(11)
 EDGE = 6
 HALF = 64
 MESH = pl.DeviceIdType.MESH
@@ -214,13 +214,14 @@
 
 
 def still_kernel(
-    n_s, n_c, features, mask, rule, first, second, cotangent,
+    n_s, n_c, features_hbm, mask_hbm, rule_hbm, first_hbm, second_hbm, cotangent_hbm,
     output, features_grad, first_grad, second_grad,
     rule_src, rule_buf, rows1_src, rows1_buf, rows2_src, rows2_buf,
     grad2_src, grad2_buf, grad1_src, grad1_buf, sum1_src, sum1_buf, sum2_src, sum2_buf,
-    back2_src, back2_buf, back1_src, back1_buf,
+    part2_src, part2_buf, part1_src, part1_buf, back2_src, back2_buf, back1_src, back1_buf,
+    features, mask, rule, cotangent, first_stack, second_stack, loads,
     faces, edges, corners, order, order_t, raw, wide1, wide2, margin,
-    ordered2, ordered1, flipped2, flipped1, running, kept_act, first_stack, second_stack,
+    ordered2, ordered1, flipped2, flipped1, running, kept_act,
     send, recv,
 ):
     me_s, me_c = lax.axis_index("space"), lax.axis_index("chan")
@@ -255,54 +256,92 @@
         for out, _ in along(kind, src_of, buf):
             out.wait_send()
 
-    def spread(kind, src, buf, act):
-        for h in range(2):
-            for c in range(n_c):
-                s = 2 * me_c + h
-
-                @pl.when(jnp.logical_not(is_me(s, c)))
-                def _():
-                    act(remote(kind, src.at[h], buf, h * n_c + c, me_s, s, c))
-
-    def spread_wait(kind, src, buf):
-        for s in range(n_s):
-
-            @pl.when(jnp.logical_not(is_me(s, me_s // 2)))
-            def _():
-                remote(kind, src.at[0], buf, 0, s, s, me_s // 2).wait_recv()
+    def if_other(s, c, act, here=None):
+        pl.when(jnp.logical_not(is_me(s, c)))(act)
+        if here is not None:
+            pl.when(is_me(s, c))(here)
 
     def spread_start(kind, src, buf):
         for h in range(2):
-
-            @pl.when(me_s == 2 * me_c + h)
-            def _():
+            s, c = 2 * me_c + h, me_s % n_c
+
+            def here():
                 buf[me_s] = src[h]
 
-        spread(kind, src, buf, lambda copy: copy.start())
-
-    def owners(kind, src, buf, act):
-        slot = (me_s % 2) * n_c + me_c
-        for s in range(n_s):
-
-            @pl.when(jnp.logical_not(is_me(s, me_s // 2)))
-            def _():
-                act(remote(kind, src.at[s], buf, s, slot, s, me_s // 2))
-
-    def owners_start(kind, src, buf):
-        @pl.when(me_s // 2 == me_c)
-        def _():
-            buf[(me_s % 2) * n_c + me_c] = src[me_s]
-
-        owners(kind, src, buf, lambda copy: copy.start())
+            if_other(s, c, lambda: remote(kind, src.at[h], buf, h, me_s, s, c).start(), here)
+
+    def handed_on(kind, buf, act):
+        for u in range(2):
+            slot = me_c + n_c * u
+            for k in range(1, n_c):
+                c = lax.rem(me_c + k, n_c)
+                act(remote(kind, buf.at[slot], buf, 2 + u * (n_c - 1) + k - 1, slot, me_s, c))
+
+    def spread_relay(kind, src, buf):
+        for u in range(2):
+            s, c = me_c + n_c * u, me_s // 2
+            if_other(s, c, lambda: remote(kind, src.at[0], buf, 0, s, s, c).wait_recv())
+        handed_on(kind, buf, lambda copy: copy.start())
+
+    def spread_wait(kind, src, buf):
+        for u in range(2):
+            for k in range(1, n_c):
+                c = lax.rem(me_c + k, n_c)
+                slot = c + n_c * u
+                remote(kind, src.at[0], buf, 0, slot, me_s, c).wait_recv()
+
+    def spread_sent(kind, src, buf):
+        for h in range(2):
+            s, c = 2 * me_c + h, me_s % n_c
+            if_other(s, c, lambda: remote(kind, src.at[h], buf, h, me_s, s, c).wait_send())
+        handed_on(kind, buf, lambda copy: copy.wait_send())
+
+    def parts(kind, src, buf, act):
+        for k in range(1, n_c):
+            c = lax.rem(me_c + k, n_c)
+            act(remote(kind, src.at[c], buf, k, me_c, me_s, c))
+
+    def owners(kind, src, buf, act, here=None):
+        for u in range(2):
+            s, c = me_c + n_c * u, me_s // 2
+
+            def keep():
+                buf[me_s % 2] = src[u]
+
+            if_other(
+                s, c, lambda: act(remote(kind, src.at[u], buf, u, me_s % 2, s, c)), keep if here else None
+            )
+
+    def parts_start(kind, src, buf):
+        buf[me_c] = src[me_c]
+        parts(kind, src, buf, lambda copy: copy.start())
+
+    def parts_relay(kind, src, buf, next_kind, next_src, next_buf):
+        for k in range(1, n_c):
+            c = lax.rem(me_c + k, n_c)
+            remote(kind, src.at[c], buf, k, c, me_s, c).wait_recv()
+        total = buf[0].astype(f32)
+        for c in range(1, n_c):
+            total = total + buf[c].astype(f32)
+        next_src[...] = total
+        owners(next_kind, next_src, next_buf, lambda copy: copy.start(), True)
 
     def owners_wait(kind, src, buf):
         for h in range(2):
-            for c in range(n_c):
-                s = 2 * me_c + h
-
-                @pl.when(jnp.logical_not(is_me(s, c)))
-                def _():
-                    remote(kind, src.at[0], buf, 0, h * n_c + c, s, c).wait_recv()
+            s, c = 2 * me_c + h, me_s % n_c
+            if_other(s, c, lambda: remote(kind, src.at[0], buf, 0, h, s, c).wait_recv())
+
+    fetched = [
+        pltpu.make_async_copy(src, dst, loads.at[i])
+        for i, (src, dst) in enumerate(
+            (
+                (mask_hbm, mask), (features_hbm, features), (cotangent_hbm, cotangent), (rule_hbm, rule),
+                (first_hbm, first_stack.at[:, 0:3]), (second_hbm, second_stack.at[:, 0:3]),
+            )
+        )
+    ]
+    for copy in fetched:
+        copy.start()
 
     barrier = pltpu.get_barrier_semaphore()
 
@@ -311,18 +350,16 @@
 
     for k in range(1, n_s):
         greet(lax.rem(me_s + k, n_s), me_c)
-    for s in range(n_s):
-
-        @pl.when(jnp.logical_not(is_me(s, me_s // 2)))
-        def _():
-            greet(s, me_s // 2)
-
+    for k in range(1, n_c):
+        greet(me_s, lax.rem(me_c + k, n_c))
     for h in range(2):
-        for c in range(n_c):
-
-            @pl.when(jnp.logical_not(is_me(2 * me_c + h, c)))
-            def _():
-                greet(2 * me_c + h, c)
+        s, c = 2 * me_c + h, me_s % n_c
+        if_other(s, c, lambda: greet(s, c))
+        s, c = me_c + n_c * h, me_s // 2
+        if_other(s, c, lambda: greet(s, c))
+
+    for copy in fetched[:4]:
+        copy.wait()
 
     square = (128, 128)
     diagonal = lax.broadcasted_iota(jnp.int32, square, 0) == lax.broadcasted_iota(jnp.int32, square, 1)
@@ -342,7 +379,7 @@
     rule_src[...] = own_rule
     rule_buf[me_s] = own_rule
 
-    greeted = n_s - 1 + n_s + 2 * n_c - 2 * jnp.where(me_s // 2 == me_c, 1, 0)
+    greeted = n_s + n_c + 2 - 2 * jnp.where(is_me(2 * me_c + me_s % 2, me_s % n_c), 1, 0)
     pl.semaphore_wait(barrier, greeted)
     start_along(RULE, lambda s: rule_src, rule_buf)
     spread_start(ROWS1, rows1_src, rows1_buf)
@@ -359,10 +396,9 @@
         return carry
 
     lax.fori_loop(0, rows // 16, order_step, 0)
-    for weight, stack in ((first, first_stack), (second, second_stack)):
-        for q in range(9):
-            stack[q, 0:192, :] = weight[3 * q : 3 * q + 3].reshape(192, 128)
-            stack[q, 192:256, :] = jnp.zeros((64, 128), bf16)
+    for stack in (first_stack, second_stack):
+        stack[:, 3] = jnp.zeros((9, 64, 128), bf16)
+    spread_relay(ROWS1, rows1_src, rows1_buf)
 
     wait_along(RULE, lambda s: rule_src, rule_buf)
     whole_rule = rule_buf[0]
@@ -422,17 +458,14 @@
             total = jnp.zeros((chunk, 128), f32)
             for q in range(9):
                 total = total + jnp.dot(
-                    taps(wide, i + q // 3, 1, q % 3), weight[q], preferred_element_type=f32
+                    taps(wide, i + q // 3, 1, q % 3), weight[q].reshape(256, 128), preferred_element_type=f32
                 )
             running[pl.ds(pl.multiple_of(i * chunk, chunk), chunk), :] = total.astype(bf16)
             return carry
 
         lax.fori_loop(0, 4, step, 0)
-        for s in range(n_s):
-            block = jnp.dot(
-                order_t[s * 128 : (s + 1) * 128, :], running[...], preferred_element_type=f32
-            ).astype(bf16)
-            target[s] = block
+        whole = jnp.dot(order_t[...], running[...], preferred_element_type=f32)
+        target[...] = whole.astype(bf16).reshape(n_s, 128, 128)
         buf[me_s] = target[me_s]
 
     def reorder(buf, ordered, flipped):
@@ -448,7 +481,7 @@
 
         def step(q, carry):
             dx, dy = q // 3, q % 3
-            kernel = weight[q]
+            kernel = weight[q].reshape(256, 128)
             for i in range(4):
                 part = lax.dot_general(
                     ordered[i * chunk : (i + 1) * chunk, :], kernel,
@@ -480,14 +513,10 @@
             margin[owner] += (got + turned(got)).reshape(margin[owner].shape)
         running[...] = margin[1:5, 1:5, 1:5].reshape(rows, 128).astype(bf16)
 
-        def back(s, carry):
-            at = pl.multiple_of(s * 128, 128)
-            got = jnp.dot(order_t[pl.ds(at, 128), :], running[...], preferred_element_type=f32)
-            upper, lower = got[:64], got[64:]
-            target[s] = jnp.where(low_lanes(upper.shape), upper, lower).astype(bf16)
-            return carry
-
-        lax.fori_loop(0, n_s, back, 0)
+        got = jnp.dot(order_t[...], running[...], preferred_element_type=f32)
+        for s in range(n_s):
+            upper, lower = got[s * 128 : s * 128 + 64], got[s * 128 + 64 : s * 128 + 128]
+            target[s % n_c, s // n_c] = jnp.where(low_lanes(upper.shape), upper, lower).astype(bf16)
 
     def kernel_grad(wide, flipped, target):
         def step(q, carry):
@@ -504,12 +533,7 @@
         return total
 
     def returned(buf):
-        sums = []
-        for h in range(2):
-            total = buf[h * n_c].astype(f32)
-            for c in range(1, n_c):
-                total = total + buf[h * n_c + c].astype(f32)
-            sums.append(total)
+        sums = (buf[0], buf[1])
         low = low_lanes(sums[0].shape)
         return jnp.concatenate(
             [
@@ -519,14 +543,16 @@
             0,
         )
 
+    for copy in fetched[4:]:
+        copy.wait()
     spread_wait(ROWS1, rows1_src, rows1_buf)
     widen(rows1_buf, wide1)
     convolve(wide1, first_stack, sum1_src, sum1_buf)
     start_along(SUM1, lambda s: sum1_src.at[s], sum1_buf)
     wait_along(GRAD2, lambda s: grad2_src, grad2_buf)
     reorder(grad2_buf, ordered2, flipped2)
-    transposed(ordered2, second_stack, back2_src)
-    owners_start(BACK2, back2_src, back2_buf)
+    transposed(ordered2, second_stack, part2_src)
+    parts_start(PART2, part2_src, part2_buf)
 
     wait_along(SUM1, lambda s: sum1_src.at[s], sum1_buf)
     act = active * summed(sum1_buf)
@@ -535,6 +561,8 @@
         rows2_src[h] = part.astype(bf16)
     spread_start(ROWS2, rows2_src, rows2_buf)
     kept_act[...] = act
+    parts_relay(PART2, part2_src, part2_buf, BACK2, back2_src, back2_buf)
+    spread_relay(ROWS2, rows2_src, rows2_buf)
 
     owners_wait(BACK2, back2_src, back2_buf)
     act = kept_act[...]
@@ -550,10 +578,11 @@
     start_along(SUM2, lambda s: sum2_src.at[s], sum2_buf)
     wait_along(GRAD1, lambda s: grad1_src, grad1_buf)
     reorder(grad1_buf, ordered1, flipped1)
-    transposed(ordered1, first_stack, back1_src)
-    owners_start(BACK1, back1_src, back1_buf)
+    transposed(ordered1, first_stack, part1_src)
+    parts_start(PART1, part1_src, part1_buf)
 
     kernel_grad(wide2, flipped2, second_grad)
+    parts_relay(PART1, part1_src, part1_buf, BACK1, back1_src, back1_buf)
     kernel_grad(wide1, flipped1, first_grad)
 
     wait_along(SUM2, lambda s: sum2_src.at[s], sum2_buf)
@@ -566,8 +595,10 @@
     sent_along(GRAD1, lambda s: grad1_src, grad1_buf)
     sent_along(SUM1, lambda s: sum1_src.at[s], sum1_buf)
     sent_along(SUM2, lambda s: sum2_src.at[s], sum2_buf)
-    spread(ROWS1, rows1_src, rows1_buf, lambda copy: copy.wait_send())
-    spread(ROWS2, rows2_src, rows2_buf, lambda copy: copy.wait_send())
+    spread_sent(ROWS1, rows1_src, rows1_buf)
+    spread_sent(ROWS2, rows2_src, rows2_buf)
+    parts(PART2, part2_src, part2_buf, lambda copy: copy.wait_send())
+    parts(PART1, part1_src, part1_buf, lambda copy: copy.wait_send())
     owners(BACK2, back2_src, back2_buf, lambda copy: copy.wait_send())
     owners(BACK1, back1_src, back1_buf, lambda copy: copy.wait_send())
 
@@ -577,7 +608,7 @@
     f32, bf16 = jnp.float32, jnp.bfloat16
 
     def stacked(weight):
-        return jnp.transpose(weight, (1, 0, 2))
+        return jnp.transpose(weight, (1, 0, 2)).reshape(9, 3, 64, 128)
 
     def buffers(shape, kind, sources=None):
         return [pltpu.VMEM(sources or shape, kind), pltpu.VMEM(shape, kind)]
@@ -589,7 +620,17 @@
         + buffers(packed, bf16, (2, 64, 128)) * 2
         + buffers(square, bf16, (128, 128)) * 2
         + buffers(square, bf16) * 2
-        + buffers(packed, bf16) * 2
+        + buffers((n_c, 2, 64, 128), bf16) * 2
+        + buffers((2, 64, 128), f32) * 2
+        + [
+            pltpu.VMEM((128, 128), bf16),
+            pltpu.VMEM((1, 128), jnp.int32),
+            pltpu.VMEM((2, 27), jnp.int32),
+            pltpu.VMEM((128, 128), bf16),
+            pltpu.VMEM((9, 4, 64, 128), bf16),
+            pltpu.VMEM((9, 4, 64, 128), bf16),
+            pltpu.SemaphoreType.DMA((6,)),
+        ]
         + [
             pltpu.VMEM((6, 256, 256), bf16),
             pltpu.VMEM((12, 64, 64), bf16),
@@ -606,21 +647,19 @@
             pltpu.VMEM((128, rows), bf16),
             pltpu.VMEM((rows, 128), bf16),
             pltpu.VMEM((128, 128), f32),
-            pltpu.VMEM((9, 256, 128), bf16),
-            pltpu.VMEM((9, 256, 128), bf16),
-            pltpu.SemaphoreType.DMA((9, max(n_s, 2 * n_c))),
-            pltpu.SemaphoreType.DMA((9, max(n_s, 2 * n_c))),
+            pltpu.SemaphoreType.DMA((11, max(n_s, 2 * n_c))),
+            pltpu.SemaphoreType.DMA((11, max(n_s, 2 * n_c))),
         ]
     )
     output, features_grad, first_grad, second_grad = pl.pallas_call(
         functools.partial(still_kernel, n_s, n_c),
         out_shape=[jax.ShapeDtypeStruct((128, 128), bf16)] * 2
         + [jax.ShapeDtypeStruct((27, 64, 128), f32)] * 2,
-        in_specs=[pl.BlockSpec(memory_space=pltpu.VMEM)] * 6,
+        in_specs=[pl.BlockSpec(memory_space=pltpu.HBM)] * 6,
         out_specs=[pl.BlockSpec(memory_space=pltpu.VMEM)] * 4,
         scratch_shapes=scratch,
         compiler_params=pltpu.CompilerParams(
-            collective_id=0, has_side_effects=True, vmem_limit_bytes=48 * 2**20
+            collective_id=0, has_side_effects=True, vmem_limit_bytes=61 * 2**20
         ),
     )(
         features, mask.reshape(1, 128), rulebook,

time: 66.1 us -> 63.4 us (0.959)
  the two profiles are of different devices: /device:TPU:0 before, /device:TPU:5 now
where the time goes in v3:
time: 63.4 us; the launch traced here: 63.2 us
  Pallas kernels  57.4 us (91%)
  local copies, waits for them, and re-layouts  5.17 us (8%)
  between operations  0.65 us (1%)
    pallas_call x1, Pallas kernels, still_weights(): pl.pallas_call(functools.partial(still_kernel, n_s, n_c), out_shape=[jax....  57.4 us
    unnamed x8, local copies, waits for them, and re-layouts  5.17 us

profile of v3, /device:TPU:5, one launch (start us, length us, event | category | flops | bytes accessed | tf_op | source)
XLA Modules:
  0.0 63.2 jit_solution(10361631605177090068)
XLA Ops:
  0.6 57.4 %shard_map.93 = (bf16[128,128]{1,0:T(8,128)(2,1)}, bf16[128,128]{1,0:T(8,128)(2,1)}, f32[27,64,128]{2,1,0:T(8,128)}, f32[27,64,128]{2,1,0:T(8,128)}) custom-call(bf16[128,128]{1,0:T(8,128)(2,1)} %features_hbm.1, s32[1,128]{1,0:T(1,128)} %bitcast.13, s32[2,27]{1,0:T(2,128)} %rule_hbm.1, bf16[9,3,64,128]{3,2,1,0:T(8,128)(2,1)} %bitcast.11, ...), custom_call_target="tpu_custom_call" | custom-call | tf_op jit(solution)/shard_map/pallas_call | solution.py:654
  58.0 0.0 copy-start.1
  58.0 1.4 %copy.14 = bf16[128,128]{1,0:T(8,128)(2,1)} copy(bf16[128,128]{1,0:T(8,128)(2,1)} %get-tuple-element.16) | data formatting | bytes 65536
  59.4 0.0 copy-done.1
  59.4 0.6 copy.15
  60.0 0.0 copy-start
  60.0 2.3 %copy.16 = f32[64,27,128]{2,0,1:T(8,128)} copy(f32[64,27,128]{2,0,1:T(8,128)} %bitcast.10) | data formatting | bytes 1769472
  62.3 0.0 copy-done
  62.3 0.9 %copy.17 = f32[64,27,128]{2,0,1:T(8,128)} copy(f32[64,27,128]{2,0,1:T(8,128)S(1)} %bitcast.9) | data formatting | bytes 1769472
Async XLA Ops:
  58.0 1.4 %copy-start.1 = (bf16[128,128]{1,0:T(8,128)(2,1)S(1)}, bf16[128,128]{1,0:T(8,128)(2,1)}, u32[]{:S(2)}) copy-start(bf16[128,128]{1,0:T(8,128)(2,1)} %get-tuple-element.17) | copy-start | bytes 98308
  60.0 2.3 %copy-start = (f32[27,64,128]{2,1,0:T(8,128)S(1)}, f32[27,64,128]{2,1,0:T(8,128)}, u32[]{:S(2)}) copy-start(f32[27,64,128]{2,1,0:T(8,128)} %get-tuple-element.11) | copy-start | bytes 2654212
